TPU v7x, 256 devices: a whole 4x4x8 slice. The times are simulated.
256 devices in a mesh: sub: 32 (over y, z), grp: 8 (over x, core).
Axes of the slice: x: 4, y: 4, z: 8, core: 2. Of those that a mesh axis runs over, the one named last changes fastest.
Arguments:
- stiffness: bfloat16 [32, 128, 5, 256, 256], P('sub', 'grp'), may hold values from -0.0009765625 to 0.0009765625
- deflation: bfloat16 [32, 64, 32768], P('sub', None, 'grp'), may hold values from -6 to 6
- off_map: int32 [32, 3], replicated, may hold values from -2 to 2, as said below
- need_map: int32 [32, 8, 3, 4], P(None, 'grp'), may hold values from 0 to 15, as said below
- place_map: int32 [32, 8, 3, 4], P('sub', 'grp'), may hold values from 0 to 15, as said below
Outputs:
- coarse: float32 [32, 256, 256], P('sub', 'grp')
Inputs may be any that keep to these rules, and one draw needn't show every extreme that they name: `off_map`: the 3 offsets of one row are distinct and nonzero. `need_map`: the 4 tile numbers of one row are distinct. `place_map`: the 4 tile numbers of one row are distinct.
All inputs are finite; a program needn't handle non-finite values.
Results may differ from a plain program's by a relative error of at most 0.0029.
Values may be sent and summed in bfloat16 or wider, within the bound.
No kernel may reach another device: no remote copies, remote signals or barrier semaphores. Data moves between devices by JAX's collectives and lax.ppermute only.
A program may use at most 128 MiB of HBM per device.

v0:
```python
import jax
import jax.numpy as jnp
from jax import lax
from jax.sharding import PartitionSpec as P

RCH = 2


def passed_along(value, axis, steps):
    count = lax.axis_size(axis)
    pairs = [(source, (source + steps) % count) for source in range(count)]
    return lax.ppermute(value, axis, pairs)


def with_halo(block, sides, width):
    for axis, dim in sides:
        count = lax.axis_size(axis)
        forward = [(i, i + 1) for i in range(count - 1)]
        backward = [(target, source) for source, target in forward]
        low = lax.ppermute(
            lax.slice_in_dim(block, block.shape[dim] - width, None, axis=dim), axis, forward
        )
        high = lax.ppermute(lax.slice_in_dim(block, 0, width, axis=dim), axis, backward)
        block = jnp.concatenate([low, block, high], axis=dim)
    return block


def slot_position(offset_value, reach_tiles):
    return jnp.where(offset_value > 0, offset_value + reach_tiles - 1, offset_value + reach_tiles)


def on_device(stiffness, deflation, off_map, need_map, place_map):
    my_index = lax.axis_index("sub")
    tile_count = stiffness.shape[1]
    band_count = stiffness.shape[2]
    tile_rows = stiffness.shape[3]
    vectors = deflation.shape[1]
    slot_count = off_map.shape[1]
    reach_tiles = RCH
    rim_tiles = band_count // 2
    own_tiles = deflation[0].reshape(vectors, tile_count, tile_rows)
    my_offsets = off_map[my_index]
    my_place = place_map[0, 0]
    offsets = [value for value in range(-reach_tiles, reach_tiles + 1) if value != 0]
    gathered = []
    arrived = []
    for offset in offsets:
        arrived.append(passed_along(own_tiles, "sub", -offset))
    stacked = jnp.stack(arrived, 0)
    my_need = need_map[my_index, 0]
    for slot_index in range(slot_count):
        position = slot_position(my_offsets[slot_index], reach_tiles)
        source = lax.dynamic_index_in_dim(stacked, position, 0, keepdims=False)
        gathered.append(jnp.take(source, my_need[slot_index], axis=1))
    neighbour_blocks = []
    for slot_index in range(slot_count):
        blank_tiles = jnp.zeros((vectors, tile_count, tile_rows), own_tiles.dtype)
        neighbour_blocks.append(
            blank_tiles.at[:, my_place[slot_index], :].set(gathered[slot_index])
        )
    layered = jnp.concatenate([own_tiles] + neighbour_blocks, 0)
    padded = with_halo(layered, (("grp", 1),), rim_tiles)
    running = jnp.zeros(layered.shape, jnp.float32)
    for band_index in range(band_count):
        window = padded[:, band_index : band_index + tile_count]
        running = running + jnp.einsum(
            "ctk,tjk->ctj", window, stiffness[0, :, band_index], preferred_element_type=jnp.float32
        )
    product_image = running.astype(jnp.bfloat16)
    columns = layered.shape[0]
    flat_basis = layered.reshape(columns, -1)
    flat_image = product_image.reshape(columns, -1)
    share = lax.psum_scatter(
        lax.dot_general(
            flat_basis, flat_image, (((1,), (1,)), ((), ())), preferred_element_type=jnp.float32
        ),
        "grp",
        scatter_dimension=0,
        tiled=True,
    )
    return share[None]


def solution(mesh):
    in_specs = (
        P("sub", "grp", None, None, None),
        P("sub", None, "grp"),
        P(),
        P(None, "grp", None, None),
        P("sub", "grp", None, None),
    )
    out_specs = P("sub", "grp", None)
    return jax.shard_map(
        on_device, mesh=mesh, in_specs=in_specs, out_specs=out_specs, check_vma=False
    )
```

profile of v0, /device:TPU:16, one launch (start us, length us, event | category | flops | bytes accessed | tf_op | source)
XLA Modules:
  0.0 127.7 jit_solution(4810752505151817823)
XLA Ops:
  6.5 1.2 copy.21
  7.7 6.3 %collective-permute-start.3 = (bf16[64,16,256]{2,1,0:T(8,128)(2,1)S(1)}, bf16[64,16,256]{2,1,0:T(8,128)(2,1)S(1)}, u32[]{:S(2)}, u32[]{:S(2)}) collective-permute-start(bf16[64,16,256]{2,1,0:T(8,128)(2,1)S(1)} %bitcast.82), channel_id=1, source_target_pairs={{0,240},{8,248},{16,0},{24,8},{32,16},{40,24},{48,32},{56,40},{64,... | collective-permute-start | bytes 1572872 | tf_op jit(solution)/shard_map/ppermute | solution.py:12
  14.0 1.0 collective-permute-start.2
  15.0 1.0 collective-permute-start.1
  16.0 0.5 collective-permute-start
  16.4 0.9 dynamic-slice_reduce_fusion
  17.5 0.6 fusion.35
  23.9 0.7 fusion.29
  24.6 0.2 copy_dynamic-update-slice_fusion
  24.7 12.1 %collective-permute-done.3 = bf16[64,16,256]{2,1,0:T(8,128)(2,1)S(1)} collective-permute-done((bf16[64,16,256]{2,1,0:T(8,128)(2,1)S(1)}, bf16[64,16,256]{2,1,0:T(8,128)(2,1)S(1)}, u32[]{:S(2)}, u32[]{:S(2)}) %collective-permute-start.3) | collective-permute-done | bytes 524320 | tf_op jit(solution)/shard_map/ppermute | solution.py:12
  36.9 10.9 %collective-permute-done.2 = bf16[64,16,256]{2,1,0:T(8,128)(2,1)} collective-permute-done((bf16[64,16,256]{2,1,0:T(8,128)(2,1)S(1)}, bf16[64,16,256]{2,1,0:T(8,128)(2,1)}, u32[]{:S(2)}, u32[]{:S(2)}) %collective-permute-start.2) | collective-permute-done | bytes 524320 | tf_op jit(solution)/shard_map/ppermute | solution.py:12
  47.7 3.5 %collective-permute-done = bf16[64,16,256]{2,1,0:T(8,128)(2,1)} collective-permute-done((bf16[64,16,256]{2,1,0:T(8,128)(2,1)S(1)}, bf16[64,16,256]{2,1,0:T(8,128)(2,1)}, u32[]{:S(2)}, u32[]{:S(2)}) %collective-permute-start) | collective-permute-done | bytes 524320 | tf_op jit(solution)/shard_map/ppermute | solution.py:12
  51.2 1.6 %pad_maximum_fusion.2 = bf16[4,64,16,256]{3,2,1,0:T(8,128)(2,1)S(1)} fusion(bf16[1,64,16,256]{3,2,1,0:T(8,128)(2,1)S(1)} %bitcast.89, bf16[1,64,16,256]{3,2,1,0:T(8,128)(2,1)} %bitcast.4, bf16[1,64,16,256]{3,2,1,0:T(8,128)(2,1)} %bitcast.3, bf16[1,64,16,256]{3,2,1,0:T(8,128)(2,1)} %bitcast.2), kind=kLoop, calls=%fused_computation.11 | loop fusion | flops 3145728 | bytes 4194304 | tf_op jit(solution)/shard_map/stack | solution.py:49
  52.8 0.1 constant_dynamic-slice_fusion
  52.9 0.2 copy.26
  53.1 1.1 copy_bitcast_fusion
  54.2 1.6 %gather_fusion.2 = bf16[4,64,256]{2,1,0:T(8,128)(2,1)S(1)} fusion(bf16[64,16,256]{2,0,1:T(8,128)(2,1)} %get-tuple-element.24, s32[1024]{0:T(1024)S(1)} %pad_clamp_fusion), kind=kCustom, calls=%fused_computation.2.clone | custom fusion | bytes 262160 | tf_op jit(solution)/shard_map/jit(_take)/gather | solution.py:54
  55.9 0.1 broadcast_select_fusion
  55.9 0.6 gather_fusion.1
  56.5 0.1 broadcast_select_fusion.1
  56.6 0.6 gather_fusion
  57.3 0.6 scatter_fusion
  58.0 0.6 scatter_fusion.1
  58.8 0.6 scatter_fusion.2
  59.5 1.3 %collective-permute-start.5 = (bf16[256,2,256]{2,0,1:T(8,128)(2,1)S(1)}, bf16[256,2,256]{2,0,1:T(8,128)(2,1)S(1)}, u32[]{:S(2)}, u32[]{:S(2)}) collective-permute-start(bf16[256,2,256]{2,0,1:T(8,128)(2,1)S(1)} %get-tuple-element.10), channel_id=1, source_target_pairs={{1,0},{2,1},{3,2},{4,3},{5,4},{6,5},{7,6},{9,8},{10,9},{11,10},{12... | collective-permute-start | bytes 786440 | tf_op jit(solution)/shard_map/ppermute | solution.py:23
  60.9 3.4 %collective-permute-start.4 = (bf16[256,2,256]{2,0,1:T(8,128)(2,1)S(1)}, bf16[256,2,256]{2,0,1:T(8,128)(2,1)S(1)}, u32[]{:S(2)}, u32[]{:S(2)}) collective-permute-start(bf16[256,2,256]{2,0,1:T(8,128)(2,1)S(1)} %get-tuple-element.9), channel_id=1, source_target_pairs={{0,1},{1,2},{2,3},{3,4},{4,5},{5,6},{6,7},{8,9},{9,10},{10,11},{11... | collective-permute-start | bytes 786440 | tf_op jit(solution)/shard_map/ppermute | solution.py:20
  64.3 4.3 %fusion.3 = f32[16,256,256]{2,1,0:T(8,128)} fusion(bf16[1,16,5,256,256]{4,3,2,1,0:T(8,128)(2,1)} %param.7, bf16[256,2,256]{2,0,1:T(8,128)(2,1)S(1)} %collective-permute-done.5, bf16[256,16,256]{2,0,1:T(8,128)(2,1)S(1)} %constant_dynamic-update-slice_fusion), kind=kOutput, calls=%fused_computation.12 | convolution fusion | flops 541589504 | bytes 8650752 | tf_op jit(solution)/shard_map/ctk,tjk->ctj/dot_general | solution.py:66
  68.6 2.7 %fusion.5 = f32[16,256,256]{2,1,0:T(8,128)} fusion(bf16[1,16,5,256,256]{4,3,2,1,0:T(8,128)(2,1)S(1)} %bitcast.91, bf16[256,2,256]{2,0,1:T(8,128)(2,1)S(1)} %collective-permute-done.5, bf16[256,16,256]{2,0,1:T(8,128)(2,1)S(1)} %constant_dynamic-update-slice_fusion), kind=kOutput, calls=%fused_computation.14 | convolution fusion | flops 541589504 | bytes 8650752 | tf_op jit(solution)/shard_map/ctk,tjk->ctj/dot_general | solution.py:66
  71.4 2.7 %fusion.9 = f32[16,256,256]{2,1,0:T(8,128)} fusion(bf16[1,16,5,256,256]{4,3,2,1,0:T(8,128)(2,1)S(1)} %bitcast.91, bf16[256,16,256]{2,0,1:T(8,128)(2,1)S(1)} %constant_dynamic-update-slice_fusion, bf16[256,2,256]{2,0,1:T(8,128)(2,1)S(1)} %collective-permute-done.4), kind=kOutput, calls=%fused_computation.18 | convolution fusion | flops 541589504 | bytes 8650752 | tf_op jit(solution)/shard_map/ctk,tjk->ctj/dot_general | solution.py:66
  74.1 2.7 %fusion.11 = f32[16,256,256]{2,1,0:T(8,128)} fusion(bf16[1,16,5,256,256]{4,3,2,1,0:T(8,128)(2,1)S(1)} %bitcast.91, bf16[256,16,256]{2,0,1:T(8,128)(2,1)S(1)} %constant_dynamic-update-slice_fusion, bf16[256,2,256]{2,0,1:T(8,128)(2,1)S(1)} %collective-permute-done.4), kind=kOutput, calls=%fused_computation.20 | convolution fusion | flops 541589504 | bytes 8650752 | tf_op jit(solution)/shard_map/ctk,tjk->ctj/dot_general | solution.py:66
  76.8 8.8 %fusion.22 = f32[256,256]{1,0:T(8,128)} fusion(bf16[256,16,256]{2,0,1:T(8,128)(2,1)S(1)} %constant_dynamic-update-slice_fusion, f32[16,256,256]{2,1,0:T(8,128)} %fusion.3, f32[16,256,256]{2,1,0:T(8,128)} %fusion.5, f32[16,256,256]{2,1,0:T(8,128)} %fusion.11, f32[16,256,256]{2,1,0:T(8,128)} %fusion.9, bf16[1,16,5,256,256]{4,3,2,1,0:T(8,128)(2,1)} %param.7), kind=kOutput, calls=%fused_computation.27 | convolution fusion | flops 1078984704 | bytes 23330816 | tf_op jit(solution)/shard_map/dot_general | solution.py:74
  85.6 35.3 %reduce-scatter.2.cloned.1.call-done = f32[32,256]{1,0:T(8,128)} async-done(((f32[256,256]{1,0:T(8,128)}), f32[32,256]{1,0:T(8,128)}) %reduce-scatter.2.cloned.1.call-update) | async-done | bytes 32784 | tf_op jit(solution)/shard_map/reduce_scatter | solution.py:73
  (30 shorter events, 0.5 us)
Async XLA Ops:
  6.5 10.9 %copy-start = (s32[32,3]{0,1:T(4,128)S(1)}, s32[32,3]{0,1:T(4,128)}, u32[]{:S(2)}) copy-start(s32[32,3]{0,1:T(4,128)} %param.9) | copy-start | bytes 1156
  6.5 114.3 %reduce-scatter.2.cloned.1.call-start = ((), (), s32[]{:S(2)}) async-start(), calls=%async_computation.1 | async-start | bytes 294912 | tf_op jit(solution)/shard_map/reduce_scatter | solution.py:73
  7.7 29.2 %collective-permute-start.3 = (bf16[64,16,256]{2,1,0:T(8,128)(2,1)S(1)}, bf16[64,16,256]{2,1,0:T(8,128)(2,1)S(1)}, u32[]{:S(2)}, u32[]{:S(2)}) collective-permute-start(bf16[64,16,256]{2,1,0:T(8,128)(2,1)S(1)} %bitcast.82), channel_id=1, source_target_pairs={{0,240},{8,248},{16,0},{24,8},{32,16},{40,24},{48,32},{56,40},{64,... | collective-permute-start | bytes 1572872 | tf_op jit(solution)/shard_map/ppermute | solution.py:12
  14.0 33.8 %collective-permute-start.2 = (bf16[64,16,256]{2,1,0:T(8,128)(2,1)S(1)}, bf16[64,16,256]{2,1,0:T(8,128)(2,1)}, u32[]{:S(2)}, u32[]{:S(2)}) collective-permute-start(bf16[64,16,256]{2,1,0:T(8,128)(2,1)S(1)} %bitcast.83), channel_id=1, source_target_pairs={{0,248},{8,0},{16,8},{24,16},{32,24},{40,32},{48,40},{56,48},{64,5... | collective-permute-start | bytes 1572872 | tf_op jit(solution)/shard_map/ppermute | solution.py:12
  15.0 32.8 %collective-permute-start.1 = (bf16[64,16,256]{2,1,0:T(8,128)(2,1)S(1)}, bf16[64,16,256]{2,1,0:T(8,128)(2,1)}, u32[]{:S(2)}, u32[]{:S(2)}) collective-permute-start(bf16[64,16,256]{2,1,0:T(8,128)(2,1)S(1)} %bitcast.84), channel_id=1, source_target_pairs={{0,8},{8,16},{16,24},{24,32},{32,40},{40,48},{48,56},{56,64},{64,7... | collective-permute-start | bytes 1572872 | tf_op jit(solution)/shard_map/ppermute | solution.py:12
  16.0 35.2 %collective-permute-start = (bf16[64,16,256]{2,1,0:T(8,128)(2,1)S(1)}, bf16[64,16,256]{2,1,0:T(8,128)(2,1)}, u32[]{:S(2)}, u32[]{:S(2)}) collective-permute-start(bf16[64,16,256]{2,1,0:T(8,128)(2,1)S(1)} %bitcast.85), channel_id=1, source_target_pairs={{0,16},{8,24},{16,32},{24,40},{32,48},{40,56},{48,64},{56,72},{64,... | collective-permute-start | bytes 1572872 | tf_op jit(solution)/shard_map/ppermute | solution.py:12
  59.5 4.8 %collective-permute-start.5 = (bf16[256,2,256]{2,0,1:T(8,128)(2,1)S(1)}, bf16[256,2,256]{2,0,1:T(8,128)(2,1)S(1)}, u32[]{:S(2)}, u32[]{:S(2)}) collective-permute-start(bf16[256,2,256]{2,0,1:T(8,128)(2,1)S(1)} %get-tuple-element.10), channel_id=1, source_target_pairs={{1,0},{2,1},{3,2},{4,3},{5,4},{6,5},{7,6},{9,8},{10,9},{11,10},{12... | collective-permute-start | bytes 786440 | tf_op jit(solution)/shard_map/ppermute | solution.py:23
  60.8 7.8 %slice-start = ((s8[10485760]{0:T(1024)(128)(4,1)}), s8[4194304]{0:T(1024)(128)(4,1)S(1)}, s32[]{:S(2)}) async-start(s8[10485760]{0:T(1024)(128)(4,1)} %bitcast.90), calls=%async_computation.2 | async-start | bytes 8388608
  60.8 7.8 %slice-start.1 = ((s8[10485760]{0:T(1024)(128)(4,1)}), s8[4194304]{0:T(1024)(128)(4,1)S(1)}, s32[]{:S(2)}) async-start(s8[10485760]{0:T(1024)(128)(4,1)} %bitcast.90), calls=%async_computation.3 | async-start | bytes 8388608
  60.9 7.8 %slice-start.2 = ((s8[10485760]{0:T(1024)(128)(4,1)}), s8[2097152]{0:T(1024)(128)(4,1)S(1)}, s32[]{:S(2)}) async-start(s8[10485760]{0:T(1024)(128)(4,1)} %bitcast.90), calls=%async_computation.4 | async-start | bytes 4194304
  60.9 10.5 %collective-permute-start.4 = (bf16[256,2,256]{2,0,1:T(8,128)(2,1)S(1)}, bf16[256,2,256]{2,0,1:T(8,128)(2,1)S(1)}, u32[]{:S(2)}, u32[]{:S(2)}) collective-permute-start(bf16[256,2,256]{2,0,1:T(8,128)(2,1)S(1)} %get-tuple-element.9), channel_id=1, source_target_pairs={{0,1},{1,2},{2,3},{3,4},{4,5},{5,6},{6,7},{8,9},{9,10},{10,11},{11... | collective-permute-start | bytes 786440 | tf_op jit(solution)/shard_map/ppermute | solution.py:20
Sparse Core Ops, SparseCore 0:
  85.7 35.0 reduce-scatter.1
where the time goes:
time: 128 us
  waiting for transfers between devices  61.7 us (48%)
  matrix products  21.2 us (17%)
  between operations  19.4 us (15%)
  starting transfers between devices  13.5 us (11%)
  local copies, waits for them, and re-layouts  9.26 us (7%)
  other arithmetic  2.6 us (2%)
    reduce_scatter x1, waiting for transfers between devices, on_device(): lax.psum_scatter(lax.dot_general(flat_basis, flat_image, (((1,), (1,)), (...  35.3 us
    ppermute x4, waiting for transfers between devices, passed_along(): return lax.ppermute(value, axis, pairs)  26.4 us
    dot_general x4, matrix products, on_device(): jnp.einsum('ctk,tjk->ctj', window, stiffness[0, :, band_index], preferred...  12.4 us
    dot_general x1, matrix products, on_device(): lax.dot_general(flat_basis, flat_image, (((1,), (1,)), ((), ())), preferr...  8.81 us
    ppermute x4, starting transfers between devices, passed_along(): return lax.ppermute(value, axis, pairs)  8.75 us
    ppermute x1, starting transfers between devices, with_halo(): lax.ppermute(lax.slice_in_dim(block, block.shape[dim] - width, None, axis...  3.44 us
    gather x3, local copies, waits for them, and re-layouts, on_device(): gathered.append(jnp.take(source, my_need[slot_index], axis=1))  2.7 us
  transfers between devices with their start and end apart: 7, of which 4 were waited for; matrix products, arithmetic and copies ran while one was open for 7% of the time, Pallas kernels for 0%

commit v1 on v0

v1 whole, which is shorter than its diff:
```python
import jax
import jax.numpy as jnp
from jax import lax
from jax.experimental import pallas as pl
from jax.experimental.pallas import tpu as pltpu
from jax.sharding import PartitionSpec as P

SUBS = 32
LAYERS = 8
TILE = 256
TD = 16
NVEC = 64
NB = 3
OV = 4
BAND = 5
RIM = BAND // 2
COLS = 256
REST = NB * NVEC
SHIFTS = (2, 1, -1, -2)
SMEM = pl.BlockSpec(memory_space=pltpu.SMEM)
VMEM = pl.BlockSpec(memory_space=pltpu.VMEM)
HBM = pl.BlockSpec(memory_space=pltpu.HBM)
NT = (((1,), (1,)), ((), ()))
bf16, f32 = jnp.bfloat16, jnp.float32


def kernel_call(body, out_shape, specs, scratch=(), mib=4, flops=0, size=0):
    return pl.pallas_call(
        body,
        out_shape=out_shape,
        in_specs=specs,
        out_specs=jax.tree.map(lambda _: VMEM, out_shape),
        scratch_shapes=scratch,
        compiler_params=pltpu.CompilerParams(vmem_limit_bytes=mib * 2**20),
        cost_estimate=pl.CostEstimate(flops=flops, bytes_accessed=size, transcendentals=0),
    )


def lanes(tile, count=1):
    return pl.ds(pl.multiple_of(tile * TILE, TILE), count * TILE)


def tile_of(ref, c):
    return ref[:, c * TILE : (c + 1) * TILE]


def row_sum(ref, stiff, c):
    total = None
    for t in range(max(0, c - RIM), min(TD, c + RIM + 1)):
        term = jnp.dot(tile_of(ref, t), stiff[t, c - t + RIM], preferred_element_type=f32)
        total = term if total is None else total + term
    return total


def pack_kernel(off_hbm, need_hbm, own_hbm, *refs):
    outs, (off_ref, need_ref, own_ref, sems) = refs[:4], refs[4:]
    copies = [
        pltpu.make_async_copy(source, target, sems.at[i])
        for i, (source, target) in enumerate(
            ((off_hbm, off_ref), (need_hbm, need_ref), (own_hbm, own_ref))
        )
    ]
    for copy in copies:
        copy.start()
    for copy in copies:
        copy.wait()
    me = lax.axis_index("sub")
    for shift, out in zip(SHIFTS, outs):
        target = lax.rem(me + (shift + SUBS), SUBS)
        slot = jnp.where(
            off_ref[0, target] == -shift, 0, jnp.where(off_ref[1, target] == -shift, 1, 2)
        )
        for o in range(OV):
            out[:, o * TILE : (o + 1) * TILE] = own_ref[:, lanes(need_ref[slot, o, target])]


def own_kernel(stiff, own, product):
    for c in range(-RIM, TD + RIM):
        product[:, (c + RIM) * TILE : (c + RIM + 1) * TILE] = row_sum(own, stiff, c).astype(bf16)


def edge_kernel(off_ref, place_ref, own, *refs):
    arrived, (near, far, sides) = refs[:4], refs[4:]
    me = lax.axis_index("sub")
    odd = lax.rem(lax.axis_index("grp"), 2)
    sides[:, NVEC:] = jnp.zeros((2, REST, RIM * TILE), bf16)
    sides[1 - odd, :NVEC] = own[:, : RIM * TILE]
    sides[odd, :NVEC] = own[:, (TD - RIM) * TILE :]
    for shift, block in zip(SHIFTS, arrived):
        first, second, third = (off_ref[slot, me] == -shift for slot in range(NB))
        slot = jnp.where(first, 0, jnp.where(second, 1, 2))
        used = jnp.logical_or(first, jnp.logical_or(second, third))
        rows = pl.ds(pl.multiple_of((slot + 1) * NVEC, NVEC), NVEC)
        for o in range(OV):
            tile = place_ref[slot, 0, o]
            low, high = tile < RIM, tile >= TD - RIM

            @pl.when(jnp.logical_and(used, jnp.logical_or(low, high)))
            def _():
                side = jnp.where(low, 1 - odd, odd)
                sides[side, rows, lanes(jnp.where(low, tile, tile - (TD - RIM)))] = tile_of(
                    block, o
                )

    near[...] = sides[0]
    far[...] = sides[1]


def main_kernel(off_ref, place_ref, stiff, own, product, *refs):
    arrived, (total, carry, basis, rows) = refs[:4], refs[4:]
    me = lax.axis_index("sub")
    basis[:NVEC] = own[...]
    basis[NVEC:] = jnp.zeros((REST, TD * TILE), bf16)
    for shift, block in zip(SHIFTS, arrived):
        for slot in range(NB):

            @pl.when(off_ref[slot, me] == -shift)
            def _():
                for o in range(OV):
                    tile = place_ref[slot, 0, o]
                    basis[(slot + 1) * NVEC : (slot + 2) * NVEC, lanes(tile)] = tile_of(block, o)

    others = basis.at[NVEC:]
    rows[:NVEC] = product[:, RIM * TILE : (RIM + TD) * TILE]
    for c in range(TD):
        rows[NVEC:, c * TILE : (c + 1) * TILE] = row_sum(others, stiff, c).astype(bf16)
    total[...] = lax.dot_general(rows[...], basis[...], NT, preferred_element_type=f32)
    carry[:NVEC, : RIM * TILE] = product[:, : RIM * TILE]
    carry[:NVEC, RIM * TILE :] = product[:, (RIM + TD) * TILE :]
    for i, c in enumerate((-2, -1, TD, TD + 1)):
        carry[NVEC:, i * TILE : (i + 1) * TILE] = row_sum(others, stiff, c).astype(bf16)


def finish_kernel(total, carry, near, far, mine, other, sums):
    odd = lax.rem(lax.axis_index("grp"), 2)

    def outer(side, right):
        half = RIM * TILE
        left = carry[:, pl.ds(pl.multiple_of(side * half, half), half)]
        return lax.dot_general(left, right[...], NT, preferred_element_type=f32)

    sums[...] = total[...] + outer(1 - odd, near) + outer(odd, far)
    share = COLS // LAYERS
    for x in range(LAYERS // 2):
        mine[x] = sums[pl.ds(pl.multiple_of((2 * x + odd) * share, share), share)]
        other[x] = sums[pl.ds(pl.multiple_of((2 * x + 1 - odd) * share, share), share)]


def swapped(value, pairs):
    return lax.ppermute(value, "grp", [p for a, b in pairs for p in ((a, b), (b, a))])


def on_device(stiffness, deflation, off_map, need_map, place_map):
    stiff, own = stiffness[0], deflation[0]
    off = off_map.T
    need = need_map.transpose(1, 2, 3, 0)[0]
    place = place_map[0].transpose(1, 0, 2)
    shape = jax.ShapeDtypeStruct

    packed = kernel_call(
        pack_kernel,
        [shape((NVEC, OV * TILE), bf16)] * 4,
        [HBM] * 3,
        [
            pltpu.SMEM(off.shape, jnp.int32),
            pltpu.SMEM(need.shape, jnp.int32),
            pltpu.VMEM(own.shape, bf16),
            pltpu.SemaphoreType.DMA((3,)),
        ],
    )(off, need, own)
    arrived = [
        lax.ppermute(block, "sub", [(k, (k + shift) % SUBS) for k in range(SUBS)])
        for shift, block in zip(SHIFTS, packed)
    ]
    product = kernel_call(
        own_kernel,
        shape((NVEC, (TD + 2 * RIM) * TILE), bf16),
        [VMEM, VMEM],
        mib=16,
        flops=2 * NVEC * TD * BAND * TILE * TILE,
        size=2**20,
    )(stiff, own)
    edges = shape((COLS, RIM * TILE), bf16)
    near, far = kernel_call(
        edge_kernel,
        [edges, edges],
        [SMEM, SMEM] + [VMEM] * 5,
        [pltpu.VMEM((2, COLS, RIM * TILE), bf16)],
    )(off, place, own, *arrived)
    near = swapped(near, [(k, k + 1) for k in range(0, LAYERS, 2)])
    far = swapped(far, [(k, k + 1) for k in range(1, LAYERS - 1, 2)])
    total, carry = kernel_call(
        main_kernel,
        [shape((COLS, COLS), f32), shape((COLS, 2 * RIM * TILE), bf16)],
        [SMEM, SMEM] + [VMEM] * 7,
        [pltpu.VMEM((COLS, TD * TILE), bf16), pltpu.VMEM((COLS, TD * TILE), bf16)],
        mib=24,
        flops=2 * COLS * TD * (BAND + 1) * TILE * TILE,
        size=2**22,
    )(off, place, stiff, own, product, *arrived)
    part = shape((LAYERS // 2, COLS // LAYERS, COLS), f32)
    mine, other = kernel_call(
        finish_kernel, [part, part], [VMEM] * 4, [pltpu.VMEM((COLS, COLS), f32)]
    )(total, carry, near, far)
    both = mine + lax.ppermute(other, "grp", [(k, k ^ 1) for k in range(LAYERS)])
    chip = lax.shift_right_logical(lax.axis_index("grp"), 1)
    share = lax.dynamic_index_in_dim(both, chip, 0, keepdims=False)
    for step in (1, 3, 2):
        block = lax.dynamic_index_in_dim(both, chip ^ step, 0, keepdims=False)
        share = share + lax.ppermute(block, "grp", [(k, k ^ (2 * step)) for k in range(LAYERS)])
    return share[None]


def solution(mesh):
    in_specs = (
        P("sub", "grp", None, None, None),
        P("sub", None, "grp"),
        P(),
        P(None, "grp", None, None),
        P("sub", "grp", None, None),
    )
    out_specs = P("sub", "grp", None)
    return jax.shard_map(
        on_device, mesh=mesh, in_specs=in_specs, out_specs=out_specs, check_vma=False
    )
```

time: 128 us -> 42 us (0.33)
  waiting for transfers between devices: 61.7 us -> 8.29 us
  matrix products: 21.2 us -> 0 us
  between operations: 19.4 us -> 0.13 us
  Pallas kernels: 0 us -> 7.73 us
  starting transfers between devices: 13.5 us -> 17.5 us
  other arithmetic: 2.6 us -> 0.64 us
  local copies, waits for them, and re-layouts: 9.26 us -> 7.49 us
    reduce_scatter x1 -> x0, waiting for transfers between devices: 35.3 us -> none  [on_device(): lax.psum_scatter(lax.dot_general(flat_basis, flat_image, (((1,), (1,)), (...]
    dot_general x5 -> x0, matrix products: 21.2 us -> none  [the longest x4 12.4 us: on_device(): jnp.einsum('ctk,tjk->ctj', window, stiffness[0, :, band_index], preferred...]
    ppermute x6 -> x10, waiting for transfers between devices: 26.5 us -> 8.29 us  [the longest x3 4.9 us: on_device(): lax.ppermute(block, 'grp', [(k, k ^ 2 * step) for k in range(LAYERS)])]
    pallas_call x0 -> x5, Pallas kernels: none -> 7.73 us  [the longest x1 3.78 us: on_device(): kernel_call(main_kernel, [shape((COLS, COLS), f32), shape((COLS, 2 * RIM...]
    unnamed x12 -> x16, local copies, waits for them, and re-layouts: 1.41 us -> 7.47 us
    ppermute x6 -> x10, starting transfers between devices: 13.5 us -> 17.5 us  [the longest x4 8.75 us: on_device(): lax.ppermute(block, 'sub', [(k, (k + shift) % SUBS) for k in range(SUBS)])]
    gather x3 -> x0, local copies, waits for them, and re-layouts: 2.7 us -> none  [on_device(): gathered.append(jnp.take(source, my_need[slot_index], axis=1))]
    scatter x3 -> x0, local copies, waits for them, and re-layouts: 1.94 us -> none  [on_device(): blank_tiles.at[:, my_place[slot_index], :].set(gathered[slot_index])]
  transfers between devices with their start and end apart: 7 -> 10, of which waited for: 4 -> 4; matrix products, arithmetic and copies ran while one was open for 7% -> 0% of each run, Pallas kernels for 0% -> 14%
where the time goes in v1:
time: 42 us; the launch traced here: 41.7 us
  starting transfers between devices  17.5 us (42%)
  waiting for transfers between devices  8.29 us (20%)
  Pallas kernels  7.73 us (18%)
  local copies, waits for them, and re-layouts  7.49 us (18%)
  other arithmetic  0.64 us (2%)
    ppermute x4, starting transfers between devices, on_device(): lax.ppermute(block, 'sub', [(k, (k + shift) % SUBS) for k in range(SUBS)])  8.75 us
    unnamed x16, local copies, waits for them, and re-layouts  7.47 us
    ppermute x3, waiting for transfers between devices, on_device(): lax.ppermute(block, 'grp', [(k, k ^ 2 * step) for k in range(LAYERS)])  4.9 us
    ppermute x3, starting transfers between devices, on_device(): lax.ppermute(block, 'grp', [(k, k ^ 2 * step) for k in range(LAYERS)])  4.19 us
    pallas_call x1, Pallas kernels, on_device(): kernel_call(main_kernel, [shape((COLS, COLS), f32), shape((COLS, 2 * RIM...  3.78 us
    ppermute x1, starting transfers between devices, on_device(): lax.ppermute(other, 'grp', [(k, k ^ 1) for k in range(LAYERS)])  3.76 us
    ppermute x4, waiting for transfers between devices, on_device(): lax.ppermute(block, 'sub', [(k, (k + shift) % SUBS) for k in range(SUBS)])  2.4 us
    pallas_call x1, Pallas kernels, on_device(): kernel_call(own_kernel, shape((NVEC, (TD + 2 * RIM) * TILE), bf16), [VMEM...  1.92 us
  transfers between devices with their start and end apart: 10, of which 4 were waited for; matrix products, arithmetic and copies ran while one was open for 0% of the time, Pallas kernels for 14%

profile of v1, /device:TPU:16, one launch (start us, length us, event | category | flops | bytes accessed | tf_op | source)
XLA Modules:
  0.0 41.7 jit_solution(8247006542402746144)
XLA Ops:
  0.0 1.1 %copy-done.2 = bf16[1,64,4096]{2,1,0:T(8,128)(2,1)S(1)} copy-done((bf16[1,64,4096]{2,1,0:T(8,128)(2,1)S(1)}, bf16[1,64,4096]{2,1,0:T(8,128)(2,1)}, u32[]{:S(2)}) %copy-start.2) | copy-done | bytes 524312
  1.1 0.7 %copy-done.4 = s32[32,3]{0,1:T(4,128)S(1)} copy-done((s32[32,3]{0,1:T(4,128)S(1)}, s32[32,3]{0,1:T(4,128)}, u32[]{:S(2)}) %copy-start.4) | copy-done | bytes 408
  1.8 0.7 %copy-done.6 = s32[32,1,3,4]{0,3,2,1:T(4,128)S(1)} copy-done((s32[32,1,3,4]{0,3,2,1:T(4,128)S(1)}, s32[32,1,3,4]{0,3,2,1:T(4,128)}, u32[]{:S(2)}) %copy-start.6) | copy-done | bytes 1560
  2.4 0.8 %shard_map.56 = (bf16[64,1024]{1,0:T(8,128)(2,1)S(1)}, bf16[64,1024]{1,0:T(8,128)(2,1)S(1)}, bf16[64,1024]{1,0:T(8,128)(2,1)S(1)}, bf16[64,1024]{1,0:T(8,128)(2,1)S(1)}) custom-call(s32[3,32]{1,0:T(4,128)S(1)} %bitcast.29, s32[3,4,32]{2,1,0:T(4,128)S(1)} %bitcast.32, bf16[64,4096]{1,0:T(8,128)(2,1)S(1)} %bitcast.25), custom_call_target="tpu_custom_call" | custom-call | tf_op jit(solution)/shard_map/pallas_call | solution.py:160
  3.2 3.3 %collective-permute-start = (bf16[64,1024]{1,0:T(8,128)(2,1)S(1)}, bf16[64,1024]{1,0:T(8,128)(2,1)S(1)}, u32[]{:S(2)}, u32[]{:S(2)}) collective-permute-start(bf16[64,1024]{1,0:T(8,128)(2,1)S(1)} %get-tuple-element.15), channel_id=1, source_target_pairs={{0,16},{8,24},{16,32},{24,40},{32,48},{40,56},{48,64},{56,72},{64,... | collective-permute-start | bytes 393224 | tf_op jit(solution)/shard_map/ppermute | solution.py:172
  6.6 1.9 %collective-permute-start.1 = (bf16[64,1024]{1,0:T(8,128)(2,1)S(1)}, bf16[64,1024]{1,0:T(8,128)(2,1)S(1)}, u32[]{:S(2)}, u32[]{:S(2)}) collective-permute-start(bf16[64,1024]{1,0:T(8,128)(2,1)S(1)} %get-tuple-element.16), channel_id=1, source_target_pairs={{0,8},{8,16},{16,24},{24,32},{32,40},{40,48},{48,56},{56,64},{64,7... | collective-permute-start | bytes 393224 | tf_op jit(solution)/shard_map/ppermute | solution.py:172
  8.5 2.2 %collective-permute-start.2 = (bf16[64,1024]{1,0:T(8,128)(2,1)S(1)}, bf16[64,1024]{1,0:T(8,128)(2,1)S(1)}, u32[]{:S(2)}, u32[]{:S(2)}) collective-permute-start(bf16[64,1024]{1,0:T(8,128)(2,1)S(1)} %get-tuple-element.17), channel_id=1, source_target_pairs={{0,248},{8,0},{16,8},{24,16},{32,24},{40,32},{48,40},{56,48},{64,5... | collective-permute-start | bytes 393224 | tf_op jit(solution)/shard_map/ppermute | solution.py:172
  10.7 1.3 %collective-permute-start.3 = (bf16[64,1024]{1,0:T(8,128)(2,1)S(1)}, bf16[64,1024]{1,0:T(8,128)(2,1)S(1)}, u32[]{:S(2)}, u32[]{:S(2)}) collective-permute-start(bf16[64,1024]{1,0:T(8,128)(2,1)S(1)} %get-tuple-element.18), channel_id=1, source_target_pairs={{0,240},{8,248},{16,0},{24,8},{32,16},{40,24},{48,32},{56,40},{64,... | collective-permute-start | bytes 393224 | tf_op jit(solution)/shard_map/ppermute | solution.py:172
  12.0 4.0 %copy-done = bf16[1,16,5,256,256]{4,3,2,1,0:T(8,128)(2,1)S(1)} copy-done((bf16[1,16,5,256,256]{4,3,2,1,0:T(8,128)(2,1)S(1)}, bf16[1,16,5,256,256]{4,3,2,1,0:T(8,128)(2,1)}, u32[]{:S(2)}) %copy-start) | copy-done | bytes 10485784
  16.0 1.0 %copy-done.3 = bf16[1,64,4096]{2,1,0:T(8,128)(2,1)S(1)} copy-done((bf16[1,64,4096]{2,1,0:T(8,128)(2,1)S(1)}, bf16[1,64,4096]{2,1,0:T(8,128)(2,1)}, u32[]{:S(2)}) %copy-start.3) | copy-done | bytes 524312
  17.0 1.9 %shard_map.55.product = bf16[64,5120]{1,0:T(8,128)(2,1)S(1)} custom-call(bf16[16,5,256,256]{3,2,1,0:T(8,128)(2,1)S(1)} %bitcast.23, bf16[64,4096]{1,0:T(8,128)(2,1)S(1)} %bitcast.26), custom_call_target="tpu_custom_call" | custom-call | flops 671088640 | bytes 1048576 | tf_op jit(solution)/shard_map/pallas_call | solution.py:175
  18.9 0.0 collective-permute-done.refs_0_
  19.0 0.0 collective-permute-done.1.refs_1_
  19.0 0.0 collective-permute-done.2.refs_2_
  19.0 2.4 %collective-permute-done.3.refs_3_ = bf16[64,1024]{1,0:T(8,128)(2,1)S(1)} collective-permute-done((bf16[64,1024]{1,0:T(8,128)(2,1)S(1)}, bf16[64,1024]{1,0:T(8,128)(2,1)S(1)}, u32[]{:S(2)}, u32[]{:S(2)}) %collective-permute-start.3) | collective-permute-done | bytes 131104 | tf_op jit(solution)/shard_map/ppermute | solution.py:172
  21.4 0.0 copy-done.7
  21.4 0.8 %shard_map.58 = (bf16[256,512]{1,0:T(8,128)(2,1)S(1)}, bf16[256,512]{1,0:T(8,128)(2,1)S(1)}) custom-call(s32[3,32]{1,0:T(4,128)S(1)} %bitcast.30, s32[3,1,4]{2,1,0:T(1,128)S(1)} %bitcast.33, bf16[64,4096]{1,0:T(8,128)(2,1)S(1)} %bitcast.27, bf16[64,1024]{1,0:T(8,128)(2,1)S(1)} %collective-permute-done.refs_0_, ...), custom_call_target="tpu_custom_call" | custom-call | tf_op jit(solution)/shard_map/pallas_call | solution.py:184
  22.2 0.1 collective-permute-start.4
  22.3 0.7 %collective-permute-start.5 = (bf16[256,512]{1,0:T(8,128)(2,1)S(1)}, bf16[256,512]{1,0:T(8,128)(2,1)S(1)}, u32[]{:S(2)}, u32[]{:S(2)}) collective-permute-start(bf16[256,512]{1,0:T(8,128)(2,1)S(1)} %get-tuple-element.22), channel_id=1, source_target_pairs={{1,2},{2,1},{3,4},{4,3},{5,6},{6,5},{9,10},{10,9},{11,12},{12,11},... | collective-permute-start | bytes 786440 | tf_op jit(solution)/shard_map/ppermute | solution.py:150
  23.0 3.8 %shard_map.57 = (f32[256,256]{1,0:T(8,128)S(1)}, bf16[256,1024]{1,0:T(8,128)(2,1)S(1)}) custom-call(s32[3,32]{1,0:T(4,128)S(1)} %bitcast.31, s32[3,1,4]{2,1,0:T(1,128)S(1)} %bitcast.34, bf16[16,5,256,256]{3,2,1,0:T(8,128)(2,1)S(1)} %bitcast.24, bf16[64,4096]{1,0:T(8,128)(2,1)S(1)} %bitcast.28, bf16[64,5120]{1,0:T(8,128)(2,1)S(1)} %shard_map.55.product, ...), custom_call_target="tpu_custom_call" | custom-call | flops 3221225472 | bytes 4194304 | tf_op jit(solution)/shard_map/pallas_call | solution.py:192
  26.8 0.0 collective-permute-done.4.near
  26.8 0.0 collective-permute-done.5.far
  26.8 0.4 shard_map.59
  27.2 3.8 %collective-permute-start.6 = (f32[4,32,256]{2,1,0:T(8,128)S(1)}, f32[4,32,256]{2,1,0:T(8,128)S(1)}, u32[]{:S(2)}, u32[]{:S(2)}) collective-permute-start(f32[4,32,256]{2,1,0:T(8,128)S(1)} %get-tuple-element.24), channel_id=1, source_target_pairs={{0,1},{1,0},{2,3},{3,2},{4,5},{5,4},{6,7},{7,6},{8,9},{9,8},{10,11... | collective-permute-start | bytes 393224 | tf_op jit(solution)/shard_map/ppermute | solution.py:205
  31.0 1.0 %collective-permute-done.6 = f32[4,32,256]{2,1,0:T(8,128)S(1)} collective-permute-done((f32[4,32,256]{2,1,0:T(8,128)S(1)}, f32[4,32,256]{2,1,0:T(8,128)S(1)}, u32[]{:S(2)}, u32[]{:S(2)}) %collective-permute-start.6) | collective-permute-done | bytes 131104 | tf_op jit(solution)/shard_map/ppermute | solution.py:205
  32.0 1.6 %collective-permute-start.7 = (f32[32,256]{1,0:T(8,128)S(1)}, f32[32,256]{1,0:T(8,128)S(1)}, u32[]{:S(2)}, u32[]{:S(2)}) collective-permute-start(f32[32,256]{1,0:T(8,128)S(1)} %get-tuple-element.25), channel_id=1, source_target_pairs={{0,2},{1,3},{2,0},{3,1},{4,6},{5,7},{6,4},{7,5},{8,10},{9,11},{10,... | collective-permute-start | bytes 98312 | tf_op jit(solution)/shard_map/ppermute | solution.py:210
  33.6 2.1 %collective-permute-start.8 = (f32[32,256]{1,0:T(8,128)S(1)}, f32[32,256]{1,0:T(8,128)S(1)}, u32[]{:S(2)}, u32[]{:S(2)}) collective-permute-start(f32[32,256]{1,0:T(8,128)S(1)} %get-tuple-element.27), channel_id=1, source_target_pairs={{0,6},{1,7},{2,4},{3,5},{4,2},{5,3},{6,0},{7,1},{8,14},{9,15},{10,... | collective-permute-start | bytes 98312 | tf_op jit(solution)/shard_map/ppermute | solution.py:210
  35.7 0.5 %collective-permute-start.9 = (f32[32,256]{1,0:T(8,128)S(1)}, f32[32,256]{1,0:T(8,128)S(1)}, u32[]{:S(2)}, u32[]{:S(2)}) collective-permute-start(f32[32,256]{1,0:T(8,128)S(1)} %get-tuple-element.26), channel_id=1, source_target_pairs={{0,4},{1,5},{2,6},{3,7},{4,0},{5,1},{6,2},{7,3},{8,12},{9,13},{10,... | collective-permute-start | bytes 98312 | tf_op jit(solution)/shard_map/ppermute | solution.py:210
  36.2 0.0 collective-permute-done.7
  36.2 2.5 %collective-permute-done.8 = f32[32,256]{1,0:T(8,128)S(1)} collective-permute-done((f32[32,256]{1,0:T(8,128)S(1)}, f32[32,256]{1,0:T(8,128)S(1)}, u32[]{:S(2)}, u32[]{:S(2)}) %collective-permute-start.8) | collective-permute-done | bytes 32800 | tf_op jit(solution)/shard_map/ppermute | solution.py:210
  38.7 2.4 %collective-permute-done.9 = f32[32,256]{1,0:T(8,128)S(1)} collective-permute-done((f32[32,256]{1,0:T(8,128)S(1)}, f32[32,256]{1,0:T(8,128)S(1)}, u32[]{:S(2)}, u32[]{:S(2)}) %collective-permute-start.9) | collective-permute-done | bytes 32800 | tf_op jit(solution)/shard_map/ppermute | solution.py:210
  41.1 0.6 %fusion.2 = f32[1,32,256]{2,1,0:T(8,128)} fusion(f32[32,256]{1,0:T(8,128)S(1)} %collective-permute-done.9, f32[32,256]{1,0:T(8,128)S(1)} %collective-permute-done.8, f32[32,256]{1,0:T(8,128)S(1)} %collective-permute-done.7, f32[4,32,256]{2,1,0:T(8,128)S(1)} %add.25, s32[]{:T(128)S(6)} %select_n.13), kind=kLoop, calls=%fused_computation.3 | loop fusion | flops 24576 | bytes 163844 | tf_op jit(solution)/shard_map/broadcast_in_dim | solution.py:211
  (12 shorter events, 0.1 us)
Async XLA Ops:
  0.0 21.4 %copy-start.5 = (s32[32,3]{0,1:T(4,128)S(1)}, s32[32,3]{0,1:T(4,128)}, u32[]{:S(2)}) copy-start(s32[32,3]{0,1:T(4,128)} %param.7) | copy-start | bytes 1156
  0.0 21.4 %copy-start.7 = (s32[1,1,3,4]{3,1,2,0:T(1,128)S(1)}, s32[1,1,3,4]{3,1,2,0:T(1,128)}, u32[]{:S(2)}) copy-start(s32[1,1,3,4]{3,1,2,0:T(1,128)} %param.9) | copy-start | bytes 148
  0.0 1.1 %copy-start.2 = (bf16[1,64,4096]{2,1,0:T(8,128)(2,1)S(1)}, bf16[1,64,4096]{2,1,0:T(8,128)(2,1)}, u32[]{:S(2)}) copy-start(bf16[1,64,4096]{2,1,0:T(8,128)(2,1)} %param.6) | copy-start | bytes 1572868
  1.1 0.7 %copy-start.4 = (s32[32,3]{0,1:T(4,128)S(1)}, s32[32,3]{0,1:T(4,128)}, u32[]{:S(2)}) copy-start(s32[32,3]{0,1:T(4,128)} %param.7) | copy-start | bytes 1156
  1.8 0.7 %copy-start.6 = (s32[32,1,3,4]{0,3,2,1:T(4,128)S(1)}, s32[32,1,3,4]{0,3,2,1:T(4,128)}, u32[]{:S(2)}) copy-start(s32[32,1,3,4]{0,3,2,1:T(4,128)} %param.8) | copy-start | bytes 4612
  3.2 15.7 %collective-permute-start = (bf16[64,1024]{1,0:T(8,128)(2,1)S(1)}, bf16[64,1024]{1,0:T(8,128)(2,1)S(1)}, u32[]{:S(2)}, u32[]{:S(2)}) collective-permute-start(bf16[64,1024]{1,0:T(8,128)(2,1)S(1)} %get-tuple-element.15), channel_id=1, source_target_pairs={{0,16},{8,24},{16,32},{24,40},{32,48},{40,56},{48,64},{56,72},{64,... | collective-permute-start | bytes 393224 | tf_op jit(solution)/shard_map/ppermute | solution.py:172
  6.6 12.4 %collective-permute-start.1 = (bf16[64,1024]{1,0:T(8,128)(2,1)S(1)}, bf16[64,1024]{1,0:T(8,128)(2,1)S(1)}, u32[]{:S(2)}, u32[]{:S(2)}) collective-permute-start(bf16[64,1024]{1,0:T(8,128)(2,1)S(1)} %get-tuple-element.16), channel_id=1, source_target_pairs={{0,8},{8,16},{16,24},{24,32},{32,40},{40,48},{48,56},{56,64},{64,7... | collective-permute-start | bytes 393224 | tf_op jit(solution)/shard_map/ppermute | solution.py:172
  8.5 10.5 %collective-permute-start.2 = (bf16[64,1024]{1,0:T(8,128)(2,1)S(1)}, bf16[64,1024]{1,0:T(8,128)(2,1)S(1)}, u32[]{:S(2)}, u32[]{:S(2)}) collective-permute-start(bf16[64,1024]{1,0:T(8,128)(2,1)S(1)} %get-tuple-element.17), channel_id=1, source_target_pairs={{0,248},{8,0},{16,8},{24,16},{32,24},{40,32},{48,40},{56,48},{64,5... | collective-permute-start | bytes 393224 | tf_op jit(solution)/shard_map/ppermute | solution.py:172
  10.7 10.6 %collective-permute-start.3 = (bf16[64,1024]{1,0:T(8,128)(2,1)S(1)}, bf16[64,1024]{1,0:T(8,128)(2,1)S(1)}, u32[]{:S(2)}, u32[]{:S(2)}) collective-permute-start(bf16[64,1024]{1,0:T(8,128)(2,1)S(1)} %get-tuple-element.18), channel_id=1, source_target_pairs={{0,240},{8,248},{16,0},{24,8},{32,16},{40,24},{48,32},{56,40},{64,... | collective-permute-start | bytes 393224 | tf_op jit(solution)/shard_map/ppermute | solution.py:172
  12.0 4.0 %copy-start = (bf16[1,16,5,256,256]{4,3,2,1,0:T(8,128)(2,1)S(1)}, bf16[1,16,5,256,256]{4,3,2,1,0:T(8,128)(2,1)}, u32[]{:S(2)}) copy-start(bf16[1,16,5,256,256]{4,3,2,1,0:T(8,128)(2,1)} %param.5) | copy-start | bytes 31457284
  16.0 1.0 %copy-start.3 = (bf16[1,64,4096]{2,1,0:T(8,128)(2,1)S(1)}, bf16[1,64,4096]{2,1,0:T(8,128)(2,1)}, u32[]{:S(2)}) copy-start(bf16[1,64,4096]{2,1,0:T(8,128)(2,1)} %param.6) | copy-start | bytes 1572868
  17.0 6.0 %copy-start.1 = (bf16[1,16,5,256,256]{4,3,2,1,0:T(8,128)(2,1)S(1)}, bf16[1,16,5,256,256]{4,3,2,1,0:T(8,128)(2,1)}, u32[]{:S(2)}) copy-start(bf16[1,16,5,256,256]{4,3,2,1,0:T(8,128)(2,1)} %param.5) | copy-start | bytes 31457284
  22.2 4.6 %collective-permute-start.4 = (bf16[256,512]{1,0:T(8,128)(2,1)S(1)}, bf16[256,512]{1,0:T(8,128)(2,1)S(1)}, u32[]{:S(2)}, u32[]{:S(2)}) collective-permute-start(bf16[256,512]{1,0:T(8,128)(2,1)S(1)} %get-tuple-element.21), channel_id=1, source_target_pairs={{0,1},{1,0},{2,3},{3,2},{4,5},{5,4},{6,7},{7,6},{8,9},{9,8},{10,11... | collective-permute-start | bytes 786440 | tf_op jit(solution)/shard_map/ppermute | solution.py:150
  22.3 4.5 %collective-permute-start.5 = (bf16[256,512]{1,0:T(8,128)(2,1)S(1)}, bf16[256,512]{1,0:T(8,128)(2,1)S(1)}, u32[]{:S(2)}, u32[]{:S(2)}) collective-permute-start(bf16[256,512]{1,0:T(8,128)(2,1)S(1)} %get-tuple-element.22), channel_id=1, source_target_pairs={{1,2},{2,1},{3,4},{4,3},{5,6},{6,5},{9,10},{10,9},{11,12},{12,11},... | collective-permute-start | bytes 786440 | tf_op jit(solution)/shard_map/ppermute | solution.py:150
  27.2 4.7 %collective-permute-start.6 = (f32[4,32,256]{2,1,0:T(8,128)S(1)}, f32[4,32,256]{2,1,0:T(8,128)S(1)}, u32[]{:S(2)}, u32[]{:S(2)}) collective-permute-start(f32[4,32,256]{2,1,0:T(8,128)S(1)} %get-tuple-element.24), channel_id=1, source_target_pairs={{0,1},{1,0},{2,3},{3,2},{4,5},{5,4},{6,7},{7,6},{8,9},{9,8},{10,11... | collective-permute-start | bytes 393224 | tf_op jit(solution)/shard_map/ppermute | solution.py:205
  32.0 4.2 %collective-permute-start.7 = (f32[32,256]{1,0:T(8,128)S(1)}, f32[32,256]{1,0:T(8,128)S(1)}, u32[]{:S(2)}, u32[]{:S(2)}) collective-permute-start(f32[32,256]{1,0:T(8,128)S(1)} %get-tuple-element.25), channel_id=1, source_target_pairs={{0,2},{1,3},{2,0},{3,1},{4,6},{5,7},{6,4},{7,5},{8,10},{9,11},{10,... | collective-permute-start | bytes 98312 | tf_op jit(solution)/shard_map/ppermute | solution.py:210
  33.6 5.1 %collective-permute-start.8 = (f32[32,256]{1,0:T(8,128)S(1)}, f32[32,256]{1,0:T(8,128)S(1)}, u32[]{:S(2)}, u32[]{:S(2)}) collective-permute-start(f32[32,256]{1,0:T(8,128)S(1)} %get-tuple-element.27), channel_id=1, source_target_pairs={{0,6},{1,7},{2,4},{3,5},{4,2},{5,3},{6,0},{7,1},{8,14},{9,15},{10,... | collective-permute-start | bytes 98312 | tf_op jit(solution)/shard_map/ppermute | solution.py:210
  35.7 5.4 %collective-permute-start.9 = (f32[32,256]{1,0:T(8,128)S(1)}, f32[32,256]{1,0:T(8,128)S(1)}, u32[]{:S(2)}, u32[]{:S(2)}) collective-permute-start(f32[32,256]{1,0:T(8,128)S(1)} %get-tuple-element.26), channel_id=1, source_target_pairs={{0,4},{1,5},{2,6},{3,7},{4,0},{5,1},{6,2},{7,3},{8,12},{9,13},{10,... | collective-permute-start | bytes 98312 | tf_op jit(solution)/shard_map/ppermute | solution.py:210

commit v2 on v1

--- a/solution.py
+++ b/solution.py
@@ -16,6 +16,7 @@
 RIM = BAND // 2
 COLS = 256
 REST = NB * NVEC
+AHEAD = 8
 SHIFTS = (2, 1, -1, -2)
 SMEM = pl.BlockSpec(memory_space=pltpu.SMEM)
 VMEM = pl.BlockSpec(memory_space=pltpu.VMEM)
@@ -29,7 +30,7 @@
         body,
         out_shape=out_shape,
         in_specs=specs,
-        out_specs=jax.tree.map(lambda _: VMEM, out_shape),
+        out_specs=[VMEM] * len(out_shape),
         scratch_shapes=scratch,
         compiler_params=pltpu.CompilerParams(vmem_limit_bytes=mib * 2**20),
         cost_estimate=pl.CostEstimate(flops=flops, bytes_accessed=size, transcendentals=0),
@@ -53,7 +54,7 @@
 
 
 def pack_kernel(off_hbm, need_hbm, own_hbm, *refs):
-    outs, (off_ref, need_ref, own_ref, sems) = refs[:4], refs[4:]
+    outs, (own_ref, off_ref, need_ref, sems) = refs[:4], refs[4:]
     copies = [
         pltpu.make_async_copy(source, target, sems.at[i])
         for i, (source, target) in enumerate(
@@ -74,8 +75,17 @@
             out[:, o * TILE : (o + 1) * TILE] = own_ref[:, lanes(need_ref[slot, o, target])]
 
 
-def own_kernel(stiff, own, product):
+def own_kernel(stiff_hbm, own, product, stiff, sems):
+    copies = [
+        pltpu.make_async_copy(stiff_hbm.at[t], stiff.at[t], sems.at[t]) for t in range(TD)
+    ]
+    for copy in copies[:AHEAD]:
+        copy.start()
     for c in range(-RIM, TD + RIM):
+        if c + RIM < TD:
+            copies[c + RIM].wait()
+            if c + RIM + AHEAD < TD:
+                copies[c + RIM + AHEAD].start()
         product[:, (c + RIM) * TILE : (c + RIM + 1) * TILE] = row_sum(own, stiff, c).astype(bf16)
 
 
@@ -131,15 +141,22 @@
         carry[NVEC:, i * TILE : (i + 1) * TILE] = row_sum(others, stiff, c).astype(bf16)
 
 
-def finish_kernel(total, carry, near, far, mine, other, sums):
-    odd = lax.rem(lax.axis_index("grp"), 2)
+def finish_kernel(total, carry, far, near, mine, other, sums):
+    layer = lax.axis_index("grp")
+    odd = lax.rem(layer, 2)
+    inner = jnp.logical_and(layer > 0, layer < LAYERS - 1)
 
     def outer(side, right):
         half = RIM * TILE
         left = carry[:, pl.ds(pl.multiple_of(side * half, half), half)]
         return lax.dot_general(left, right[...], NT, preferred_element_type=f32)
 
-    sums[...] = total[...] + outer(1 - odd, near) + outer(odd, far)
+    sums[...] = total[...] + outer(1 - odd, near)
+
+    @pl.when(inner)
+    def _():
+        sums[...] += outer(odd, far)
+
     share = COLS // LAYERS
     for x in range(LAYERS // 2):
         mine[x] = sums[pl.ds(pl.multiple_of((2 * x + odd) * share, share), share)]
@@ -157,29 +174,31 @@
     place = place_map[0].transpose(1, 0, 2)
     shape = jax.ShapeDtypeStruct
 
-    packed = kernel_call(
+    *packed, own = kernel_call(
         pack_kernel,
-        [shape((NVEC, OV * TILE), bf16)] * 4,
+        [shape((NVEC, OV * TILE), bf16)] * 4 + [pltpu.VMEM(own.shape, bf16)],
         [HBM] * 3,
         [
             pltpu.SMEM(off.shape, jnp.int32),
             pltpu.SMEM(need.shape, jnp.int32),
-            pltpu.VMEM(own.shape, bf16),
             pltpu.SemaphoreType.DMA((3,)),
         ],
-    )(off, need, own)
+    )(*(pltpu.with_memory_space_constraint(value, pltpu.HBM) for value in (off, need, own)))
+    own = pltpu.with_memory_space_constraint(own, pltpu.VMEM)
     arrived = [
         lax.ppermute(block, "sub", [(k, (k + shift) % SUBS) for k in range(SUBS)])
         for shift, block in zip(SHIFTS, packed)
     ]
-    product = kernel_call(
+    product, stiff = kernel_call(
         own_kernel,
-        shape((NVEC, (TD + 2 * RIM) * TILE), bf16),
-        [VMEM, VMEM],
-        mib=16,
+        [shape((NVEC, (TD + 2 * RIM) * TILE), bf16), pltpu.VMEM(stiff.shape, bf16)],
+        [HBM, VMEM],
+        [pltpu.SemaphoreType.DMA((TD,))],
+        mib=4,
         flops=2 * NVEC * TD * BAND * TILE * TILE,
-        size=2**20,
-    )(stiff, own)
+        size=2**24,
+    )(pltpu.with_memory_space_constraint(stiff, pltpu.HBM), own)
+    stiff = pltpu.with_memory_space_constraint(stiff, pltpu.VMEM)
     edges = shape((COLS, RIM * TILE), bf16)
     near, far = kernel_call(
         edge_kernel,
@@ -187,8 +206,8 @@
         [SMEM, SMEM] + [VMEM] * 5,
         [pltpu.VMEM((2, COLS, RIM * TILE), bf16)],
     )(off, place, own, *arrived)
+    far = swapped(far, [(k, (k + 1) % LAYERS) for k in range(1, LAYERS, 2)])
     near = swapped(near, [(k, k + 1) for k in range(0, LAYERS, 2)])
-    far = swapped(far, [(k, k + 1) for k in range(1, LAYERS - 1, 2)])
     total, carry = kernel_call(
         main_kernel,
         [shape((COLS, COLS), f32), shape((COLS, 2 * RIM * TILE), bf16)],
@@ -201,11 +220,11 @@
     part = shape((LAYERS // 2, COLS // LAYERS, COLS), f32)
     mine, other = kernel_call(
         finish_kernel, [part, part], [VMEM] * 4, [pltpu.VMEM((COLS, COLS), f32)]
-    )(total, carry, near, far)
+    )(total, carry, far, near)
     both = mine + lax.ppermute(other, "grp", [(k, k ^ 1) for k in range(LAYERS)])
     chip = lax.shift_right_logical(lax.axis_index("grp"), 1)
     share = lax.dynamic_index_in_dim(both, chip, 0, keepdims=False)
-    for step in (1, 3, 2):
+    for step in (2, 3, 1):
         block = lax.dynamic_index_in_dim(both, chip ^ step, 0, keepdims=False)
         share = share + lax.ppermute(block, "grp", [(k, k ^ (2 * step)) for k in range(LAYERS)])
     return share[None]

time: 42 us -> 37 us (0.88)
  local copies, waits for them, and re-layouts: 7.49 us -> 0.02 us
  Pallas kernels: 7.73 us -> 12.2 us
  starting transfers between devices: 17.5 us -> 14.1 us
  waiting for transfers between devices: 8.29 us -> 9.9 us
    unnamed x16 -> x4, local copies, waits for them, and re-layouts: 7.47 us -> 0.01 us
    pallas_call x2, Pallas kernels: 2.7 us -> 7.31 us  [the longest x1 6.14 us: on_device(): kernel_call(own_kernel, [shape((NVEC, (TD + 2 * RIM) * TILE), bf16), pltp...]
    ppermute x1, starting transfers between devices: 3.76 us -> 0.09 us  [on_device(): lax.ppermute(other, 'grp', [(k, k ^ 1) for k in range(LAYERS)])]
    ppermute x2, waiting for transfers between devices: 0.01 us -> 1.67 us  [swapped(): lax.ppermute(value, 'grp', [p for a, b in pairs for p in ((a, b), (b, a))])]
    ppermute x3, waiting for transfers between devices: 4.9 us -> 3.69 us  [on_device(): lax.ppermute(block, 'grp', [(k, k ^ 2 * step) for k in range(LAYERS)])]
    ppermute x2, starting transfers between devices: 0.77 us -> 1.69 us  [swapped(): lax.ppermute(value, 'grp', [p for a, b in pairs for p in ((a, b), (b, a))])]
    ppermute x4, waiting for transfers between devices: 2.4 us -> 3.22 us  [on_device(): lax.ppermute(block, 'sub', [(k, (k + shift) % SUBS) for k in range(SUBS)])]
    ppermute x3, starting transfers between devices: 4.19 us -> 3.58 us  [on_device(): lax.ppermute(block, 'grp', [(k, k ^ 2 * step) for k in range(LAYERS)])]
  transfers between devices with their start and end apart: 10 -> 10, of which waited for: 4 -> 5; matrix products, arithmetic and copies ran while one was open for 0% -> 0% of each run, Pallas kernels for 14% -> 27%
where the time goes in v2:
time: 37 us; the launch traced here: 36.9 us
  starting transfers between devices  14.1 us (38%)
  Pallas kernels  12.2 us (33%)
  waiting for transfers between devices  9.9 us (27%)
  other arithmetic  0.64 us (2%)
    ppermute x4, starting transfers between devices, on_device(): lax.ppermute(block, 'sub', [(k, (k + shift) % SUBS) for k in range(SUBS)])  8.75 us
    pallas_call x1, Pallas kernels, on_device(): kernel_call(own_kernel, [shape((NVEC, (TD + 2 * RIM) * TILE), bf16), pltp...  6.14 us
    pallas_call x1, Pallas kernels, on_device(): kernel_call(main_kernel, [shape((COLS, COLS), f32), shape((COLS, 2 * RIM...  3.72 us
    ppermute x3, waiting for transfers between devices, on_device(): lax.ppermute(block, 'grp', [(k, k ^ 2 * step) for k in range(LAYERS)])  3.69 us
    ppermute x3, starting transfers between devices, on_device(): lax.ppermute(block, 'grp', [(k, k ^ 2 * step) for k in range(LAYERS)])  3.58 us
    ppermute x4, waiting for transfers between devices, on_device(): lax.ppermute(block, 'sub', [(k, (k + shift) % SUBS) for k in range(SUBS)])  3.22 us
    ppermute x2, starting transfers between devices, swapped(): lax.ppermute(value, 'grp', [p for a, b in pairs for p in ((a, b), (b, a))])  1.69 us
    ppermute x2, waiting for transfers between devices, swapped(): lax.ppermute(value, 'grp', [p for a, b in pairs for p in ((a, b), (b, a))])  1.67 us
  transfers between devices with their start and end apart: 10, of which 5 were waited for; matrix products, arithmetic and copies ran while one was open for 0% of the time, Pallas kernels for 27%

profile of v2, /device:TPU:16, one launch (start us, length us, event | category | flops | bytes accessed | tf_op | source)
XLA Modules:
  0.0 36.9 jit_solution(15304420248718536427)
XLA Ops:
  0.0 0.0 copy-start
  0.0 0.0 copy-start.1
  0.0 1.2 %shard_map.55 = (bf16[64,1024]{1,0:T(8,128)(2,1)S(1)}, bf16[64,1024]{1,0:T(8,128)(2,1)S(1)}, bf16[64,1024]{1,0:T(8,128)(2,1)S(1)}, bf16[64,1024]{1,0:T(8,128)(2,1)S(1)}, bf16[64,4096]{1,0:T(8,128)(2,1)S(1)}) custom-call(s32[3,32]{1,0:T(4,128)} %bitcast.23, s32[3,4,32]{2,1,0:T(4,128)} %bitcast.30, bf16[64,4096]{1,0:T(8,128)(2,1)} %bitcast.29), custom_call_target="tpu_custom_call" | custom-call | tf_op jit(solution)/shard_map/pallas_call | solution.py:177
  1.2 3.3 %collective-permute-start = (bf16[64,1024]{1,0:T(8,128)(2,1)S(1)}, bf16[64,1024]{1,0:T(8,128)(2,1)S(1)}, u32[]{:S(2)}, u32[]{:S(2)}) collective-permute-start(bf16[64,1024]{1,0:T(8,128)(2,1)S(1)} %get-tuple-element.21), channel_id=1, source_target_pairs={{0,16},{8,24},{16,32},{24,40},{32,48},{40,56},{48,64},{56,72},{64,... | collective-permute-start | bytes 393224 | tf_op jit(solution)/shard_map/ppermute | solution.py:189
  4.5 1.9 %collective-permute-start.1 = (bf16[64,1024]{1,0:T(8,128)(2,1)S(1)}, bf16[64,1024]{1,0:T(8,128)(2,1)S(1)}, u32[]{:S(2)}, u32[]{:S(2)}) collective-permute-start(bf16[64,1024]{1,0:T(8,128)(2,1)S(1)} %get-tuple-element.22), channel_id=1, source_target_pairs={{0,8},{8,16},{16,24},{24,32},{32,40},{40,48},{48,56},{56,64},{64,7... | collective-permute-start | bytes 393224 | tf_op jit(solution)/shard_map/ppermute | solution.py:189
  6.4 2.2 %collective-permute-start.2 = (bf16[64,1024]{1,0:T(8,128)(2,1)S(1)}, bf16[64,1024]{1,0:T(8,128)(2,1)S(1)}, u32[]{:S(2)}, u32[]{:S(2)}) collective-permute-start(bf16[64,1024]{1,0:T(8,128)(2,1)S(1)} %get-tuple-element.23), channel_id=1, source_target_pairs={{0,248},{8,0},{16,8},{24,16},{32,24},{40,32},{48,40},{56,48},{64,5... | collective-permute-start | bytes 393224 | tf_op jit(solution)/shard_map/ppermute | solution.py:189
  8.7 1.3 %collective-permute-start.3 = (bf16[64,1024]{1,0:T(8,128)(2,1)S(1)}, bf16[64,1024]{1,0:T(8,128)(2,1)S(1)}, u32[]{:S(2)}, u32[]{:S(2)}) collective-permute-start(bf16[64,1024]{1,0:T(8,128)(2,1)S(1)} %get-tuple-element.24), channel_id=1, source_target_pairs={{0,240},{8,248},{16,0},{24,8},{32,16},{40,24},{48,32},{56,40},{64,... | collective-permute-start | bytes 393224 | tf_op jit(solution)/shard_map/ppermute | solution.py:189
  9.9 6.1 %shard_map.56 = (bf16[64,5120]{1,0:T(8,128)(2,1)S(1)}, bf16[16,5,256,256]{3,2,1,0:T(8,128)(2,1)S(1)}) custom-call(bf16[16,5,256,256]{3,2,1,0:T(8,128)(2,1)} %bitcast.28, bf16[64,4096]{1,0:T(8,128)(2,1)S(1)} %get-tuple-element.18.own), custom_call_target="tpu_custom_call" | custom-call | flops 671088640 | bytes 16777216 | tf_op jit(solution)/shard_map/pallas_call | solution.py:192
  16.1 0.0 collective-permute-done.refs_0_
  16.1 0.0 collective-permute-done.1.refs_1_
  16.1 0.0 collective-permute-done.2.refs_2_
  16.1 3.2 %collective-permute-done.3.refs_3_ = bf16[64,1024]{1,0:T(8,128)(2,1)S(1)} collective-permute-done((bf16[64,1024]{1,0:T(8,128)(2,1)S(1)}, bf16[64,1024]{1,0:T(8,128)(2,1)S(1)}, u32[]{:S(2)}, u32[]{:S(2)}) %collective-permute-start.3) | collective-permute-done | bytes 131104 | tf_op jit(solution)/shard_map/ppermute | solution.py:189
  19.3 0.0 copy-done
  19.3 0.0 copy-done.1
  19.3 0.8 %shard_map.58 = (bf16[256,512]{1,0:T(8,128)(2,1)S(1)}, bf16[256,512]{1,0:T(8,128)(2,1)S(1)}) custom-call(s32[3,32]{1,0:T(4,128)S(1)} %bitcast.24, s32[3,1,4]{2,1,0:T(1,128)S(1)} %bitcast.26, bf16[64,4096]{1,0:T(8,128)(2,1)S(1)} %get-tuple-element.18.own, bf16[64,1024]{1,0:T(8,128)(2,1)S(1)} %collective-permute-done.refs_0_, ...), custom_call_target="tpu_custom_call" | custom-call | tf_op jit(solution)/shard_map/pallas_call | solution.py:203
  20.2 0.1 collective-permute-start.4
  20.3 1.6 %collective-permute-start.5 = (bf16[256,512]{1,0:T(8,128)(2,1)S(1)}, bf16[256,512]{1,0:T(8,128)(2,1)S(1)}, u32[]{:S(2)}, u32[]{:S(2)}) collective-permute-start(bf16[256,512]{1,0:T(8,128)(2,1)S(1)} %get-tuple-element.28), channel_id=1, source_target_pairs={{0,1},{1,0},{2,3},{3,2},{4,5},{5,4},{6,7},{7,6},{8,9},{9,8},{10,11... | collective-permute-start | bytes 786440 | tf_op jit(solution)/shard_map/ppermute | solution.py:167
  21.9 3.7 %shard_map.57 = (f32[256,256]{1,0:T(8,128)S(1)}, bf16[256,1024]{1,0:T(8,128)(2,1)S(1)}) custom-call(s32[3,32]{1,0:T(4,128)S(1)} %bitcast.25, s32[3,1,4]{2,1,0:T(1,128)S(1)} %bitcast.27, bf16[16,5,256,256]{3,2,1,0:T(8,128)(2,1)S(1)} %get-tuple-element.19.stiff, bf16[64,4096]{1,0:T(8,128)(2,1)S(1)} %get-tuple-element.18.own, ...), custom_call_target="tpu_custom_call" | custom-call | flops 3221225472 | bytes 4194304 | tf_op jit(solution)/shard_map/pallas_call | solution.py:211
  25.6 1.7 %collective-permute-done.4.far = bf16[256,512]{1,0:T(8,128)(2,1)S(1)} collective-permute-done((bf16[256,512]{1,0:T(8,128)(2,1)S(1)}, bf16[256,512]{1,0:T(8,128)(2,1)S(1)}, u32[]{:S(2)}, u32[]{:S(2)}) %collective-permute-start.4) | collective-permute-done | bytes 262176 | tf_op jit(solution)/shard_map/ppermute | solution.py:167
  27.3 0.0 collective-permute-done.5.near
  27.3 0.3 shard_map.59
  27.6 0.1 collective-permute-start.6
  27.7 1.3 %collective-permute-done.6 = f32[4,32,256]{2,1,0:T(8,128)S(1)} collective-permute-done((f32[4,32,256]{2,1,0:T(8,128)S(1)}, f32[4,32,256]{2,1,0:T(8,128)S(1)}, u32[]{:S(2)}, u32[]{:S(2)}) %collective-permute-start.6) | collective-permute-done | bytes 131104 | tf_op jit(solution)/shard_map/ppermute | solution.py:224
  29.0 2.1 %collective-permute-start.7 = (f32[32,256]{1,0:T(8,128)S(1)}, f32[32,256]{1,0:T(8,128)S(1)}, u32[]{:S(2)}, u32[]{:S(2)}) collective-permute-start(f32[32,256]{1,0:T(8,128)S(1)} %get-tuple-element.31), channel_id=1, source_target_pairs={{0,4},{1,5},{2,6},{3,7},{4,0},{5,1},{6,2},{7,3},{8,12},{9,13},{10,... | collective-permute-start | bytes 98312 | tf_op jit(solution)/shard_map/ppermute | solution.py:229
  31.2 1.1 %collective-permute-start.8 = (f32[32,256]{1,0:T(8,128)S(1)}, f32[32,256]{1,0:T(8,128)S(1)}, u32[]{:S(2)}, u32[]{:S(2)}) collective-permute-start(f32[32,256]{1,0:T(8,128)S(1)} %get-tuple-element.33), channel_id=1, source_target_pairs={{0,6},{1,7},{2,4},{3,5},{4,2},{5,3},{6,0},{7,1},{8,14},{9,15},{10,... | collective-permute-start | bytes 98312 | tf_op jit(solution)/shard_map/ppermute | solution.py:229
  32.3 0.3 collective-permute-start.9
  32.6 1.9 %collective-permute-done.7 = f32[32,256]{1,0:T(8,128)S(1)} collective-permute-done((f32[32,256]{1,0:T(8,128)S(1)}, f32[32,256]{1,0:T(8,128)S(1)}, u32[]{:S(2)}, u32[]{:S(2)}) %collective-permute-start.7) | collective-permute-done | bytes 32800 | tf_op jit(solution)/shard_map/ppermute | solution.py:229
  34.5 1.8 %collective-permute-done.8 = f32[32,256]{1,0:T(8,128)S(1)} collective-permute-done((f32[32,256]{1,0:T(8,128)S(1)}, f32[32,256]{1,0:T(8,128)S(1)}, u32[]{:S(2)}, u32[]{:S(2)}) %collective-permute-start.8) | collective-permute-done | bytes 32800 | tf_op jit(solution)/shard_map/ppermute | solution.py:229
  36.3 0.0 collective-permute-done.9
  36.3 0.6 %fusion.2 = f32[1,32,256]{2,1,0:T(8,128)} fusion(f32[32,256]{1,0:T(8,128)S(1)} %collective-permute-done.9, f32[32,256]{1,0:T(8,128)S(1)} %collective-permute-done.8, f32[32,256]{1,0:T(8,128)S(1)} %collective-permute-done.7, f32[4,32,256]{2,1,0:T(8,128)S(1)} %add.25, s32[]{:T(128)S(6)} %select_n.13), kind=kLoop, calls=%fused_computation.3 | loop fusion | flops 24576 | bytes 163844 | tf_op jit(solution)/shard_map/broadcast_in_dim | solution.py:230
  (2 shorter events, 0.0 us)
Async XLA Ops:
  0.0 19.3 %copy-start = (s32[32,3]{0,1:T(4,128)S(1)}, s32[32,3]{0,1:T(4,128)}, u32[]{:S(2)}) copy-start(s32[32,3]{0,1:T(4,128)} %param.7) | copy-start | bytes 1156
  0.0 19.3 %copy-start.1 = (s32[1,1,3,4]{3,1,2,0:T(1,128)S(1)}, s32[1,1,3,4]{3,1,2,0:T(1,128)}, u32[]{:S(2)}) copy-start(s32[1,1,3,4]{3,1,2,0:T(1,128)} %param.9) | copy-start | bytes 148
  1.2 14.9 %collective-permute-start = (bf16[64,1024]{1,0:T(8,128)(2,1)S(1)}, bf16[64,1024]{1,0:T(8,128)(2,1)S(1)}, u32[]{:S(2)}, u32[]{:S(2)}) collective-permute-start(bf16[64,1024]{1,0:T(8,128)(2,1)S(1)} %get-tuple-element.21), channel_id=1, source_target_pairs={{0,16},{8,24},{16,32},{24,40},{32,48},{40,56},{48,64},{56,72},{64,... | collective-permute-start | bytes 393224 | tf_op jit(solution)/shard_map/ppermute | solution.py:189
  4.5 11.6 %collective-permute-start.1 = (bf16[64,1024]{1,0:T(8,128)(2,1)S(1)}, bf16[64,1024]{1,0:T(8,128)(2,1)S(1)}, u32[]{:S(2)}, u32[]{:S(2)}) collective-permute-start(bf16[64,1024]{1,0:T(8,128)(2,1)S(1)} %get-tuple-element.22), channel_id=1, source_target_pairs={{0,8},{8,16},{16,24},{24,32},{32,40},{40,48},{48,56},{56,64},{64,7... | collective-permute-start | bytes 393224 | tf_op jit(solution)/shard_map/ppermute | solution.py:189
  6.4 9.7 %collective-permute-start.2 = (bf16[64,1024]{1,0:T(8,128)(2,1)S(1)}, bf16[64,1024]{1,0:T(8,128)(2,1)S(1)}, u32[]{:S(2)}, u32[]{:S(2)}) collective-permute-start(bf16[64,1024]{1,0:T(8,128)(2,1)S(1)} %get-tuple-element.23), channel_id=1, source_target_pairs={{0,248},{8,0},{16,8},{24,16},{32,24},{40,32},{48,40},{56,48},{64,5... | collective-permute-start | bytes 393224 | tf_op jit(solution)/shard_map/ppermute | solution.py:189
  8.7 10.6 %collective-permute-start.3 = (bf16[64,1024]{1,0:T(8,128)(2,1)S(1)}, bf16[64,1024]{1,0:T(8,128)(2,1)S(1)}, u32[]{:S(2)}, u32[]{:S(2)}) collective-permute-start(bf16[64,1024]{1,0:T(8,128)(2,1)S(1)} %get-tuple-element.24), channel_id=1, source_target_pairs={{0,240},{8,248},{16,0},{24,8},{32,16},{40,24},{48,32},{56,40},{64,... | collective-permute-start | bytes 393224 | tf_op jit(solution)/shard_map/ppermute | solution.py:189
  20.2 7.1 %collective-permute-start.4 = (bf16[256,512]{1,0:T(8,128)(2,1)S(1)}, bf16[256,512]{1,0:T(8,128)(2,1)S(1)}, u32[]{:S(2)}, u32[]{:S(2)}) collective-permute-start(bf16[256,512]{1,0:T(8,128)(2,1)S(1)} %get-tuple-element.27), channel_id=1, source_target_pairs={{1,2},{2,1},{3,4},{4,3},{5,6},{6,5},{7,0},{0,7},{9,10},{10,9},{11,... | collective-permute-start | bytes 786440 | tf_op jit(solution)/shard_map/ppermute | solution.py:167
  20.3 7.0 %collective-permute-start.5 = (bf16[256,512]{1,0:T(8,128)(2,1)S(1)}, bf16[256,512]{1,0:T(8,128)(2,1)S(1)}, u32[]{:S(2)}, u32[]{:S(2)}) collective-permute-start(bf16[256,512]{1,0:T(8,128)(2,1)S(1)} %get-tuple-element.28), channel_id=1, source_target_pairs={{0,1},{1,0},{2,3},{3,2},{4,5},{5,4},{6,7},{7,6},{8,9},{9,8},{10,11... | collective-permute-start | bytes 786440 | tf_op jit(solution)/shard_map/ppermute | solution.py:167
  27.6 1.4 %collective-permute-start.6 = (f32[4,32,256]{2,1,0:T(8,128)S(1)}, f32[4,32,256]{2,1,0:T(8,128)S(1)}, u32[]{:S(2)}, u32[]{:S(2)}) collective-permute-start(f32[4,32,256]{2,1,0:T(8,128)S(1)} %get-tuple-element.30), channel_id=1, source_target_pairs={{0,1},{1,0},{2,3},{3,2},{4,5},{5,4},{6,7},{7,6},{8,9},{9,8},{10,11... | collective-permute-start | bytes 393224 | tf_op jit(solution)/shard_map/ppermute | solution.py:224
  29.0 5.5 %collective-permute-start.7 = (f32[32,256]{1,0:T(8,128)S(1)}, f32[32,256]{1,0:T(8,128)S(1)}, u32[]{:S(2)}, u32[]{:S(2)}) collective-permute-start(f32[32,256]{1,0:T(8,128)S(1)} %get-tuple-element.31), channel_id=1, source_target_pairs={{0,4},{1,5},{2,6},{3,7},{4,0},{5,1},{6,2},{7,3},{8,12},{9,13},{10,... | collective-permute-start | bytes 98312 | tf_op jit(solution)/shard_map/ppermute | solution.py:229
  31.2 5.1 %collective-permute-start.8 = (f32[32,256]{1,0:T(8,128)S(1)}, f32[32,256]{1,0:T(8,128)S(1)}, u32[]{:S(2)}, u32[]{:S(2)}) collective-permute-start(f32[32,256]{1,0:T(8,128)S(1)} %get-tuple-element.33), channel_id=1, source_target_pairs={{0,6},{1,7},{2,4},{3,5},{4,2},{5,3},{6,0},{7,1},{8,14},{9,15},{10,... | collective-permute-start | bytes 98312 | tf_op jit(solution)/shard_map/ppermute | solution.py:229
  32.3 4.0 %collective-permute-start.9 = (f32[32,256]{1,0:T(8,128)S(1)}, f32[32,256]{1,0:T(8,128)S(1)}, u32[]{:S(2)}, u32[]{:S(2)}) collective-permute-start(f32[32,256]{1,0:T(8,128)S(1)} %get-tuple-element.32), channel_id=1, source_target_pairs={{0,2},{1,3},{2,0},{3,1},{4,6},{5,7},{6,4},{7,5},{8,10},{9,11},{10,... | collective-permute-start | bytes 98312 | tf_op jit(solution)/shard_map/ppermute | solution.py:229

commit v3 on v2

--- a/solution.py
+++ b/solution.py
@@ -17,7 +17,7 @@
 COLS = 256
 REST = NB * NVEC
 AHEAD = 8
-SHIFTS = (2, 1, -1, -2)
+SHIFTS = (2, 1, -2, -1)
 SMEM = pl.BlockSpec(memory_space=pltpu.SMEM)
 VMEM = pl.BlockSpec(memory_space=pltpu.VMEM)
 HBM = pl.BlockSpec(memory_space=pltpu.HBM)
@@ -25,13 +25,14 @@
 bf16, f32 = jnp.bfloat16, jnp.float32
 
 
-def kernel_call(body, out_shape, specs, scratch=(), mib=4, flops=0, size=0):
+def kernel_call(body, out_shape, specs, scratch=(), mib=4, flops=0, size=0, aliases=None):
     return pl.pallas_call(
         body,
         out_shape=out_shape,
         in_specs=specs,
         out_specs=[VMEM] * len(out_shape),
         scratch_shapes=scratch,
+        input_output_aliases=aliases or {},
         compiler_params=pltpu.CompilerParams(vmem_limit_bytes=mib * 2**20),
         cost_estimate=pl.CostEstimate(flops=flops, bytes_accessed=size, transcendentals=0),
     )
@@ -75,27 +76,38 @@
             out[:, o * TILE : (o + 1) * TILE] = own_ref[:, lanes(need_ref[slot, o, target])]
 
 
-def own_kernel(stiff_hbm, own, product, stiff, sems):
+def split(value):
+    first = value.astype(bf16)
+    return first, (value - first.astype(f32)).astype(bf16)
+
+
+def own_kernel(stiff_hbm, own, product, rest, stiff, basis, near, far, sems):
     copies = [
         pltpu.make_async_copy(stiff_hbm.at[t], stiff.at[t], sems.at[t]) for t in range(TD)
     ]
     for copy in copies[:AHEAD]:
         copy.start()
+    odd = lax.rem(lax.axis_index("grp"), 2)
+    basis[:NVEC] = own[...]
+    basis[NVEC:] = jnp.zeros((REST, TD * TILE), bf16)
+    for ref, first in ((near, (1 - odd) * (TD - RIM)), (far, odd * (TD - RIM))):
+        ref[:NVEC] = own[:, lanes(first, RIM)]
+        ref[NVEC:] = jnp.zeros((REST, RIM * TILE), bf16)
     for c in range(-RIM, TD + RIM):
         if c + RIM < TD:
             copies[c + RIM].wait()
             if c + RIM + AHEAD < TD:
                 copies[c + RIM + AHEAD].start()
-        product[:, (c + RIM) * TILE : (c + RIM + 1) * TILE] = row_sum(own, stiff, c).astype(bf16)
-
-
-def edge_kernel(off_ref, place_ref, own, *refs):
-    arrived, (near, far, sides) = refs[:4], refs[4:]
+        first, second = split(row_sum(own, stiff, c))
+        product[:, (c + RIM) * TILE : (c + RIM + 1) * TILE] = first
+        if 0 <= c < TD:
+            rest[:, c * TILE : (c + 1) * TILE] = second
+
+
+def edge_kernel(off_ref, place_ref, *refs):
+    arrived, (near, far) = refs[2:6], refs[6:]
     me = lax.axis_index("sub")
-    odd = lax.rem(lax.axis_index("grp"), 2)
-    sides[:, NVEC:] = jnp.zeros((2, REST, RIM * TILE), bf16)
-    sides[1 - odd, :NVEC] = own[:, : RIM * TILE]
-    sides[odd, :NVEC] = own[:, (TD - RIM) * TILE :]
+    odd = lax.rem(lax.axis_index("grp"), 2) == 1
     for shift, block in zip(SHIFTS, arrived):
         first, second, third = (off_ref[slot, me] == -shift for slot in range(NB))
         slot = jnp.where(first, 0, jnp.where(second, 1, 2))
@@ -104,23 +116,21 @@
         for o in range(OV):
             tile = place_ref[slot, 0, o]
             low, high = tile < RIM, tile >= TD - RIM
-
-            @pl.when(jnp.logical_and(used, jnp.logical_or(low, high)))
+            spot = lanes(jnp.where(low, tile, tile - (TD - RIM)))
+            rim = jnp.logical_and(used, jnp.logical_or(low, high))
+
+            @pl.when(jnp.logical_and(rim, low == odd))
             def _():
-                side = jnp.where(low, 1 - odd, odd)
-                sides[side, rows, lanes(jnp.where(low, tile, tile - (TD - RIM)))] = tile_of(
-                    block, o
-                )
-
-    near[...] = sides[0]
-    far[...] = sides[1]
-
-
-def main_kernel(off_ref, place_ref, stiff, own, product, *refs):
-    arrived, (total, carry, basis, rows) = refs[:4], refs[4:]
+                near[rows, spot] = tile_of(block, o)
+
+            @pl.when(jnp.logical_and(rim, low != odd))
+            def _():
+                far[rows, spot] = tile_of(block, o)
+
+
+def main_kernel(off_ref, place_ref, stiff, product, rest, _, *refs):
+    arrived, (total, carry, basis, rows, low_rows) = refs[:4], refs[4:]
     me = lax.axis_index("sub")
-    basis[:NVEC] = own[...]
-    basis[NVEC:] = jnp.zeros((REST, TD * TILE), bf16)
     for shift, block in zip(SHIFTS, arrived):
         for slot in range(NB):
 
@@ -132,9 +142,14 @@
 
     others = basis.at[NVEC:]
     rows[:NVEC] = product[:, RIM * TILE : (RIM + TD) * TILE]
+    low_rows[:NVEC] = rest[...]
     for c in range(TD):
-        rows[NVEC:, c * TILE : (c + 1) * TILE] = row_sum(others, stiff, c).astype(bf16)
-    total[...] = lax.dot_general(rows[...], basis[...], NT, preferred_element_type=f32)
+        first, second = split(row_sum(others, stiff, c))
+        rows[NVEC:, c * TILE : (c + 1) * TILE] = first
+        low_rows[NVEC:, c * TILE : (c + 1) * TILE] = second
+    total[...] = lax.dot_general(
+        rows[...], basis[...], NT, preferred_element_type=f32
+    ) + lax.dot_general(low_rows[...], basis[...], NT, preferred_element_type=f32)
     carry[:NVEC, : RIM * TILE] = product[:, : RIM * TILE]
     carry[:NVEC, RIM * TILE :] = product[:, (RIM + TD) * TILE :]
     for i, c in enumerate((-2, -1, TD, TD + 1)):
@@ -161,6 +176,18 @@
     for x in range(LAYERS // 2):
         mine[x] = sums[pl.ds(pl.multiple_of((2 * x + odd) * share, share), share)]
         other[x] = sums[pl.ds(pl.multiple_of((2 * x + 1 - odd) * share, share), share)]
+
+
+def far_moves():
+    moves = []
+    for sub in range(SUBS):
+        for layer in range(LAYERS):
+            if layer in (0, LAYERS - 1):
+                to = (sub ^ 1, layer)
+            else:
+                to = (sub, layer + 1 if layer % 2 else layer - 1)
+            moves.append((sub * LAYERS + layer, to[0] * LAYERS + to[1]))
+    return moves
 
 
 def swapped(value, pairs):
@@ -189,34 +216,48 @@
         lax.ppermute(block, "sub", [(k, (k + shift) % SUBS) for k in range(SUBS)])
         for shift, block in zip(SHIFTS, packed)
     ]
-    product, stiff = kernel_call(
+    edges = pltpu.VMEM((COLS, RIM * TILE), bf16)
+    whole = pltpu.VMEM((COLS, TD * TILE), bf16)
+    product, rest, *kept = kernel_call(
         own_kernel,
-        [shape((NVEC, (TD + 2 * RIM) * TILE), bf16), pltpu.VMEM(stiff.shape, bf16)],
+        [
+            shape((NVEC, (TD + 2 * RIM) * TILE), bf16),
+            shape((NVEC, TD * TILE), bf16),
+            pltpu.VMEM(stiff.shape, bf16),
+            whole,
+            edges,
+            edges,
+        ],
         [HBM, VMEM],
         [pltpu.SemaphoreType.DMA((TD,))],
-        mib=4,
         flops=2 * NVEC * TD * BAND * TILE * TILE,
         size=2**24,
     )(pltpu.with_memory_space_constraint(stiff, pltpu.HBM), own)
-    stiff = pltpu.with_memory_space_constraint(stiff, pltpu.VMEM)
-    edges = shape((COLS, RIM * TILE), bf16)
+    stiff, basis, near, far = (
+        pltpu.with_memory_space_constraint(value, pltpu.VMEM) for value in kept
+    )
     near, far = kernel_call(
         edge_kernel,
-        [edges, edges],
-        [SMEM, SMEM] + [VMEM] * 5,
-        [pltpu.VMEM((2, COLS, RIM * TILE), bf16)],
-    )(off, place, own, *arrived)
-    far = swapped(far, [(k, (k + 1) % LAYERS) for k in range(1, LAYERS, 2)])
+        [shape((COLS, RIM * TILE), bf16)] * 2,
+        [SMEM, SMEM] + [VMEM] * 6,
+        aliases={2: 0, 3: 1},
+    )(off, place, near, far, *arrived)
+    far = lax.ppermute(far, ("sub", "grp"), far_moves())
     near = swapped(near, [(k, k + 1) for k in range(0, LAYERS, 2)])
-    total, carry = kernel_call(
+    total, carry, _ = kernel_call(
         main_kernel,
-        [shape((COLS, COLS), f32), shape((COLS, 2 * RIM * TILE), bf16)],
-        [SMEM, SMEM] + [VMEM] * 7,
-        [pltpu.VMEM((COLS, TD * TILE), bf16), pltpu.VMEM((COLS, TD * TILE), bf16)],
+        [
+            shape((COLS, COLS), f32),
+            shape((COLS, 2 * RIM * TILE), bf16),
+            shape((COLS, TD * TILE), bf16),
+        ],
+        [SMEM, SMEM] + [VMEM] * 8,
+        [pltpu.VMEM((COLS, TD * TILE), bf16)] * 2,
         mib=24,
         flops=2 * COLS * TD * (BAND + 1) * TILE * TILE,
         size=2**22,
-    )(off, place, stiff, own, product, *arrived)
+        aliases={5: 2},
+    )(off, place, stiff, product, rest, basis, *arrived)
     part = shape((LAYERS // 2, COLS // LAYERS, COLS), f32)
     mine, other = kernel_call(
         finish_kernel, [part, part], [VMEM] * 4, [pltpu.VMEM((COLS, COLS), f32)]

time: 37 us -> 36.7 us (level); the launches traced: 36.9 us -> 36.1 us
  waiting for transfers between devices: 9.9 us -> 8.24 us
  Pallas kernels: 12.2 us -> 12.6 us
  starting transfers between devices: 14.1 us -> 14.5 us
    ppermute x2 -> x1, waiting for transfers between devices: 1.67 us -> 0.01 us  [swapped(): lax.ppermute(value, 'grp', [p for a, b in pairs for p in ((a, b), (b, a))])]
    ppermute x4, waiting for transfers between devices: 3.22 us -> 2.26 us  [on_device(): lax.ppermute(block, 'sub', [(k, (k + shift) % SUBS) for k in range(SUBS)])]
    ppermute x0 -> x1, starting transfers between devices: none -> 0.88 us  [on_device(): far = lax.ppermute(far, ('sub', 'grp'), far_moves())]
    ppermute x2 -> x1, starting transfers between devices: 1.69 us -> 0.81 us  [swapped(): lax.ppermute(value, 'grp', [p for a, b in pairs for p in ((a, b), (b, a))])]
    ppermute x0 -> x1, waiting for transfers between devices: none -> 0.68 us  [on_device(): far = lax.ppermute(far, ('sub', 'grp'), far_moves())]
  transfers between devices with their start and end apart: 10 -> 10, of which waited for: 5 -> 6; matrix products, arithmetic and copies ran while one was open for 0% -> 0% of each run, Pallas kernels for 27% -> 28%
where the time goes in v3:
time: 36.7 us; the launch traced here: 36.1 us
  starting transfers between devices  14.5 us (40%)
  Pallas kernels  12.6 us (34%)
  waiting for transfers between devices  8.24 us (22%)
  other arithmetic  0.64 us (2%)
    ppermute x4, starting transfers between devices, on_device(): lax.ppermute(block, 'sub', [(k, (k + shift) % SUBS) for k in range(SUBS)])  8.75 us
    pallas_call x1, Pallas kernels, on_device(): kernel_call(own_kernel, [shape((NVEC, (TD + 2 * RIM) * TILE), bf16), shap...  6.18 us
    pallas_call x1, Pallas kernels, on_device(): kernel_call(main_kernel, [shape((COLS, COLS), f32), shape((COLS, 2 * RIM...  4.08 us
    ppermute x3, waiting for transfers between devices, on_device(): lax.ppermute(block, 'grp', [(k, k ^ 2 * step) for k in range(LAYERS)])  3.99 us
    ppermute x3, starting transfers between devices, on_device(): lax.ppermute(block, 'grp', [(k, k ^ 2 * step) for k in range(LAYERS)])  3.93 us
    ppermute x4, waiting for transfers between devices, on_device(): lax.ppermute(block, 'sub', [(k, (k + shift) % SUBS) for k in range(SUBS)])  2.26 us
    ppermute x1, waiting for transfers between devices, on_device(): lax.ppermute(other, 'grp', [(k, k ^ 1) for k in range(LAYERS)])  1.31 us
    pallas_call x1, Pallas kernels, on_device(): kernel_call(pack_kernel, [shape((NVEC, OV * TILE), bf16)] * 4 + [pltpu.VM...  1.17 us
  transfers between devices with their start and end apart: 10, of which 6 were waited for; matrix products, arithmetic and copies ran while one was open for 0% of the time, Pallas kernels for 28%

profile of v3, /device:TPU:16, one launch (start us, length us, event | category | flops | bytes accessed | tf_op | source)
XLA Modules:
  0.0 36.1 jit_solution(18219911287908279971)
XLA Ops:
  0.0 0.0 copy-start
  0.0 0.0 copy-start.1
  0.0 1.2 %shard_map.55 = (bf16[64,1024]{1,0:T(8,128)(2,1)S(1)}, bf16[64,1024]{1,0:T(8,128)(2,1)S(1)}, bf16[64,1024]{1,0:T(8,128)(2,1)S(1)}, bf16[64,1024]{1,0:T(8,128)(2,1)S(1)}, bf16[64,4096]{1,0:T(8,128)(2,1)S(1)}) custom-call(s32[3,32]{1,0:T(4,128)} %bitcast.23, s32[3,4,32]{2,1,0:T(4,128)} %bitcast.30, bf16[64,4096]{1,0:T(8,128)(2,1)} %bitcast.29), custom_call_target="tpu_custom_call" | custom-call | tf_op jit(solution)/shard_map/pallas_call | solution.py:204
  1.2 3.3 %collective-permute-start = (bf16[64,1024]{1,0:T(8,128)(2,1)S(1)}, bf16[64,1024]{1,0:T(8,128)(2,1)S(1)}, u32[]{:S(2)}, u32[]{:S(2)}) collective-permute-start(bf16[64,1024]{1,0:T(8,128)(2,1)S(1)} %get-tuple-element.27), channel_id=1, source_target_pairs={{0,16},{8,24},{16,32},{24,40},{32,48},{40,56},{48,64},{56,72},{64,... | collective-permute-start | bytes 393224 | tf_op jit(solution)/shard_map/ppermute | solution.py:216
  4.5 1.9 %collective-permute-start.1 = (bf16[64,1024]{1,0:T(8,128)(2,1)S(1)}, bf16[64,1024]{1,0:T(8,128)(2,1)S(1)}, u32[]{:S(2)}, u32[]{:S(2)}) collective-permute-start(bf16[64,1024]{1,0:T(8,128)(2,1)S(1)} %get-tuple-element.28), channel_id=1, source_target_pairs={{0,8},{8,16},{16,24},{24,32},{32,40},{40,48},{48,56},{56,64},{64,7... | collective-permute-start | bytes 393224 | tf_op jit(solution)/shard_map/ppermute | solution.py:216
  6.4 2.1 %collective-permute-start.2 = (bf16[64,1024]{1,0:T(8,128)(2,1)S(1)}, bf16[64,1024]{1,0:T(8,128)(2,1)S(1)}, u32[]{:S(2)}, u32[]{:S(2)}) collective-permute-start(bf16[64,1024]{1,0:T(8,128)(2,1)S(1)} %get-tuple-element.29), channel_id=1, source_target_pairs={{0,240},{8,248},{16,0},{24,8},{32,16},{40,24},{48,32},{56,40},{64,... | collective-permute-start | bytes 393224 | tf_op jit(solution)/shard_map/ppermute | solution.py:216
  8.6 1.4 %collective-permute-start.3 = (bf16[64,1024]{1,0:T(8,128)(2,1)S(1)}, bf16[64,1024]{1,0:T(8,128)(2,1)S(1)}, u32[]{:S(2)}, u32[]{:S(2)}) collective-permute-start(bf16[64,1024]{1,0:T(8,128)(2,1)S(1)} %get-tuple-element.30), channel_id=1, source_target_pairs={{0,248},{8,0},{16,8},{24,16},{32,24},{40,32},{48,40},{56,48},{64,5... | collective-permute-start | bytes 393224 | tf_op jit(solution)/shard_map/ppermute | solution.py:216
  9.9 6.2 %shard_map.56 = (bf16[64,5120]{1,0:T(8,128)(2,1)S(1)}, bf16[64,4096]{1,0:T(8,128)(2,1)S(1)}, bf16[16,5,256,256]{3,2,1,0:T(8,128)(2,1)S(1)}, bf16[256,4096]{1,0:T...) custom-call(bf16[16,5,256,256]{3,2,1,0:T(8,128)(2,1)} %bitcast.28, ...), custom_call_target="tpu_custom_call" | custom-call | flops 671088640 | bytes 16777216 | tf_op jit(solution)/shard_map/pallas_call | solution.py:221
  16.1 0.0 collective-permute-done.refs_0_.refs_2_
  16.1 0.0 collective-permute-done.1.refs_1_.refs_3_
  16.1 0.2 collective-permute-done.2.refs_2_.refs_4_
  16.3 2.1 %collective-permute-done.3.refs_3_.refs_5_ = bf16[64,1024]{1,0:T(8,128)(2,1)S(1)} collective-permute-done((bf16[64,1024]{1,0:T(8,128)(2,1)S(1)}, bf16[64,1024]{1,0:T(8,128)(2,1)S(1)}, u32[]{:S(2)}, u32[]{:S(2)}) %collective-permute-start.3) | collective-permute-done | bytes 131104 | tf_op jit(solution)/shard_map/ppermute | solution.py:216
  18.4 0.0 copy-done
  18.4 0.0 copy-done.1
  18.4 0.9 %shard_map.58 = (bf16[256,512]{1,0:T(8,128)(2,1)S(1)}, bf16[256,512]{1,0:T(8,128)(2,1)S(1)}) custom-call(s32[3,32]{1,0:T(4,128)S(1)} %bitcast.24, s32[3,1,4]{2,1,0:T(1,128)S(1)} %bitcast.26, bf16[256,512]{1,0:T(8,128)(2,1)S(1)} %get-tuple-element.33.refs_0_, ...), custom_call_target="tpu_custom_call", output_to_operand_aliasing={{0}: (2, {}), {1}: (3, {})} | custom-call | tf_op jit(solution)/shard_map/pallas_call | solution.py:239
  19.3 0.9 %collective-permute-start.4 = (bf16[256,512]{1,0:T(8,128)(2,1)S(1)}, bf16[256,512]{1,0:T(8,128)(2,1)S(1)}, u32[]{:S(2)}, u32[]{:S(2)}) collective-permute-start(bf16[256,512]{1,0:T(8,128)(2,1)S(1)} %get-tuple-element.35), channel_id=1, source_target_pairs={{0,8},{1,2},{2,1},{3,4},{4,3},{5,6},{6,5},{7,15},{8,0},{9,10},{10,... | collective-permute-start | bytes 786440 | tf_op jit(solution)/shard_map/ppermute | solution.py:245
  20.2 0.8 %collective-permute-start.5 = (bf16[256,512]{1,0:T(8,128)(2,1)S(1)}, bf16[256,512]{1,0:T(8,128)(2,1)S(1)}, u32[]{:S(2)}, u32[]{:S(2)}) collective-permute-start(bf16[256,512]{1,0:T(8,128)(2,1)S(1)} %get-tuple-element.36), channel_id=1, source_target_pairs={{0,1},{1,0},{2,3},{3,2},{4,5},{5,4},{6,7},{7,6},{8,9},{9,8},{10,11... | collective-permute-start | bytes 786440 | tf_op jit(solution)/shard_map/ppermute | solution.py:194
  21.0 4.1 %shard_map.57 = (f32[256,256]{1,0:T(8,128)S(1)}, bf16[256,1024]{1,0:T(8,128)(2,1)S(1)}, bf16[256,4096]{1,0:T(8,128)(2,1)S(1)}) custom-call(s32[3,32]{1,0:T(4,128)S(1)} %bitcast.25, s32[3,1,4]{2,1,0:T(1,128)S(1)} %bitcast.27, bf16[16,5,256,256]{3,2,1,0:T(8,128)(2,1)S(1)} %get-tuple-element.23.stiff, ...), custom_call_target="tpu_custom_call", output_to_operand_aliasing={{2}: (5, {})} | custom-call | flops 3221225472 | bytes 4194304 | tf_op jit(solution)/shard_map/pallas_call | solution.py:247
  25.1 0.7 %collective-permute-done.4.far = bf16[256,512]{1,0:T(8,128)(2,1)S(1)} collective-permute-done((bf16[256,512]{1,0:T(8,128)(2,1)S(1)}, bf16[256,512]{1,0:T(8,128)(2,1)S(1)}, u32[]{:S(2)}, u32[]{:S(2)}) %collective-permute-start.4) | collective-permute-done | bytes 262176 | tf_op jit(solution)/shard_map/ppermute | solution.py:245
  25.8 0.0 collective-permute-done.5.near
  25.8 0.3 shard_map.59
  26.1 0.1 collective-permute-start.6
  26.2 1.3 %collective-permute-done.6 = f32[4,32,256]{2,1,0:T(8,128)S(1)} collective-permute-done((f32[4,32,256]{2,1,0:T(8,128)S(1)}, f32[4,32,256]{2,1,0:T(8,128)S(1)}, u32[]{:S(2)}, u32[]{:S(2)}) %collective-permute-start.6) | collective-permute-done | bytes 131104 | tf_op jit(solution)/shard_map/ppermute | solution.py:265
  27.6 2.8 %collective-permute-start.7 = (f32[32,256]{1,0:T(8,128)S(1)}, f32[32,256]{1,0:T(8,128)S(1)}, u32[]{:S(2)}, u32[]{:S(2)}) collective-permute-start(f32[32,256]{1,0:T(8,128)S(1)} %get-tuple-element.39), channel_id=1, source_target_pairs={{0,4},{1,5},{2,6},{3,7},{4,0},{5,1},{6,2},{7,3},{8,12},{9,13},{10,... | collective-permute-start | bytes 98312 | tf_op jit(solution)/shard_map/ppermute | solution.py:270
  30.4 1.1 %collective-permute-start.8 = (f32[32,256]{1,0:T(8,128)S(1)}, f32[32,256]{1,0:T(8,128)S(1)}, u32[]{:S(2)}, u32[]{:S(2)}) collective-permute-start(f32[32,256]{1,0:T(8,128)S(1)} %get-tuple-element.41), channel_id=1, source_target_pairs={{0,6},{1,7},{2,4},{3,5},{4,2},{5,3},{6,0},{7,1},{8,14},{9,15},{10,... | collective-permute-start | bytes 98312 | tf_op jit(solution)/shard_map/ppermute | solution.py:270
  31.5 0.0 collective-permute-start.9
  31.5 1.6 %collective-permute-done.7 = f32[32,256]{1,0:T(8,128)S(1)} collective-permute-done((f32[32,256]{1,0:T(8,128)S(1)}, f32[32,256]{1,0:T(8,128)S(1)}, u32[]{:S(2)}, u32[]{:S(2)}) %collective-permute-start.7) | collective-permute-done | bytes 32800 | tf_op jit(solution)/shard_map/ppermute | solution.py:270
  33.1 2.4 %collective-permute-done.8 = f32[32,256]{1,0:T(8,128)S(1)} collective-permute-done((f32[32,256]{1,0:T(8,128)S(1)}, f32[32,256]{1,0:T(8,128)S(1)}, u32[]{:S(2)}, u32[]{:S(2)}) %collective-permute-start.8) | collective-permute-done | bytes 32800 | tf_op jit(solution)/shard_map/ppermute | solution.py:270
  35.5 0.0 collective-permute-done.9
  35.5 0.6 %fusion.2 = f32[1,32,256]{2,1,0:T(8,128)} fusion(f32[32,256]{1,0:T(8,128)S(1)} %collective-permute-done.9, f32[32,256]{1,0:T(8,128)S(1)} %collective-permute-done.8, f32[32,256]{1,0:T(8,128)S(1)} %collective-permute-done.7, f32[4,32,256]{2,1,0:T(8,128)S(1)} %add.25, s32[]{:T(128)S(6)} %select_n.13), kind=kLoop, calls=%fused_computation.3 | loop fusion | flops 24576 | bytes 163844 | tf_op jit(solution)/shard_map/broadcast_in_dim | solution.py:271
  (2 shorter events, 0.0 us)
Async XLA Ops:
  0.0 18.4 %copy-start = (s32[32,3]{0,1:T(4,128)S(1)}, s32[32,3]{0,1:T(4,128)}, u32[]{:S(2)}) copy-start(s32[32,3]{0,1:T(4,128)} %param.7) | copy-start | bytes 1156
  0.0 18.4 %copy-start.1 = (s32[1,1,3,4]{3,1,2,0:T(1,128)S(1)}, s32[1,1,3,4]{3,1,2,0:T(1,128)}, u32[]{:S(2)}) copy-start(s32[1,1,3,4]{3,1,2,0:T(1,128)} %param.9) | copy-start | bytes 148
  1.2 14.9 %collective-permute-start = (bf16[64,1024]{1,0:T(8,128)(2,1)S(1)}, bf16[64,1024]{1,0:T(8,128)(2,1)S(1)}, u32[]{:S(2)}, u32[]{:S(2)}) collective-permute-start(bf16[64,1024]{1,0:T(8,128)(2,1)S(1)} %get-tuple-element.27), channel_id=1, source_target_pairs={{0,16},{8,24},{16,32},{24,40},{32,48},{40,56},{48,64},{56,72},{64,... | collective-permute-start | bytes 393224 | tf_op jit(solution)/shard_map/ppermute | solution.py:216
  4.5 11.6 %collective-permute-start.1 = (bf16[64,1024]{1,0:T(8,128)(2,1)S(1)}, bf16[64,1024]{1,0:T(8,128)(2,1)S(1)}, u32[]{:S(2)}, u32[]{:S(2)}) collective-permute-start(bf16[64,1024]{1,0:T(8,128)(2,1)S(1)} %get-tuple-element.28), channel_id=1, source_target_pairs={{0,8},{8,16},{16,24},{24,32},{32,40},{40,48},{48,56},{56,64},{64,7... | collective-permute-start | bytes 393224 | tf_op jit(solution)/shard_map/ppermute | solution.py:216
  6.4 9.9 %collective-permute-start.2 = (bf16[64,1024]{1,0:T(8,128)(2,1)S(1)}, bf16[64,1024]{1,0:T(8,128)(2,1)S(1)}, u32[]{:S(2)}, u32[]{:S(2)}) collective-permute-start(bf16[64,1024]{1,0:T(8,128)(2,1)S(1)} %get-tuple-element.29), channel_id=1, source_target_pairs={{0,240},{8,248},{16,0},{24,8},{32,16},{40,24},{48,32},{56,40},{64,... | collective-permute-start | bytes 393224 | tf_op jit(solution)/shard_map/ppermute | solution.py:216
  8.6 9.8 %collective-permute-start.3 = (bf16[64,1024]{1,0:T(8,128)(2,1)S(1)}, bf16[64,1024]{1,0:T(8,128)(2,1)S(1)}, u32[]{:S(2)}, u32[]{:S(2)}) collective-permute-start(bf16[64,1024]{1,0:T(8,128)(2,1)S(1)} %get-tuple-element.30), channel_id=1, source_target_pairs={{0,248},{8,0},{16,8},{24,16},{32,24},{40,32},{48,40},{56,48},{64,5... | collective-permute-start | bytes 393224 | tf_op jit(solution)/shard_map/ppermute | solution.py:216
  19.3 6.5 %collective-permute-start.4 = (bf16[256,512]{1,0:T(8,128)(2,1)S(1)}, bf16[256,512]{1,0:T(8,128)(2,1)S(1)}, u32[]{:S(2)}, u32[]{:S(2)}) collective-permute-start(bf16[256,512]{1,0:T(8,128)(2,1)S(1)} %get-tuple-element.35), channel_id=1, source_target_pairs={{0,8},{1,2},{2,1},{3,4},{4,3},{5,6},{6,5},{7,15},{8,0},{9,10},{10,... | collective-permute-start | bytes 786440 | tf_op jit(solution)/shard_map/ppermute | solution.py:245
  20.2 5.6 %collective-permute-start.5 = (bf16[256,512]{1,0:T(8,128)(2,1)S(1)}, bf16[256,512]{1,0:T(8,128)(2,1)S(1)}, u32[]{:S(2)}, u32[]{:S(2)}) collective-permute-start(bf16[256,512]{1,0:T(8,128)(2,1)S(1)} %get-tuple-element.36), channel_id=1, source_target_pairs={{0,1},{1,0},{2,3},{3,2},{4,5},{5,4},{6,7},{7,6},{8,9},{9,8},{10,11... | collective-permute-start | bytes 786440 | tf_op jit(solution)/shard_map/ppermute | solution.py:194
  26.1 1.4 %collective-permute-start.6 = (f32[4,32,256]{2,1,0:T(8,128)S(1)}, f32[4,32,256]{2,1,0:T(8,128)S(1)}, u32[]{:S(2)}, u32[]{:S(2)}) collective-permute-start(f32[4,32,256]{2,1,0:T(8,128)S(1)} %get-tuple-element.38), channel_id=1, source_target_pairs={{0,1},{1,0},{2,3},{3,2},{4,5},{5,4},{6,7},{7,6},{8,9},{9,8},{10,11... | collective-permute-start | bytes 393224 | tf_op jit(solution)/shard_map/ppermute | solution.py:265
  27.6 5.5 %collective-permute-start.7 = (f32[32,256]{1,0:T(8,128)S(1)}, f32[32,256]{1,0:T(8,128)S(1)}, u32[]{:S(2)}, u32[]{:S(2)}) collective-permute-start(f32[32,256]{1,0:T(8,128)S(1)} %get-tuple-element.39), channel_id=1, source_target_pairs={{0,4},{1,5},{2,6},{3,7},{4,0},{5,1},{6,2},{7,3},{8,12},{9,13},{10,... | collective-permute-start | bytes 98312 | tf_op jit(solution)/shard_map/ppermute | solution.py:270
  30.4 5.1 %collective-permute-start.8 = (f32[32,256]{1,0:T(8,128)S(1)}, f32[32,256]{1,0:T(8,128)S(1)}, u32[]{:S(2)}, u32[]{:S(2)}) collective-permute-start(f32[32,256]{1,0:T(8,128)S(1)} %get-tuple-element.41), channel_id=1, source_target_pairs={{0,6},{1,7},{2,4},{3,5},{4,2},{5,3},{6,0},{7,1},{8,14},{9,15},{10,... | collective-permute-start | bytes 98312 | tf_op jit(solution)/shard_map/ppermute | solution.py:270
  31.5 4.0 %collective-permute-start.9 = (f32[32,256]{1,0:T(8,128)S(1)}, f32[32,256]{1,0:T(8,128)S(1)}, u32[]{:S(2)}, u32[]{:S(2)}) collective-permute-start(f32[32,256]{1,0:T(8,128)S(1)} %get-tuple-element.40), channel_id=1, source_target_pairs={{0,2},{1,3},{2,0},{3,1},{4,6},{5,7},{6,4},{7,5},{8,10},{9,11},{10,... | collective-permute-start | bytes 98312 | tf_op jit(solution)/shard_map/ppermute | solution.py:270

commit v4 on v3

--- a/solution.py
+++ b/solution.py
@@ -17,7 +17,7 @@
 COLS = 256
 REST = NB * NVEC
 AHEAD = 8
-SHIFTS = (2, 1, -2, -1)
+SHIFTS = (1, 2, -2, -1)
 SMEM = pl.BlockSpec(memory_space=pltpu.SMEM)
 VMEM = pl.BlockSpec(memory_space=pltpu.VMEM)
 HBM = pl.BlockSpec(memory_space=pltpu.HBM)

time: 36.7 us -> 36.6 us (level)
  no operation moved by 1% of the time
where the time goes in v4:
time: 36.6 us; the launch traced here: 36.1 us
  starting transfers between devices  14.6 us (40%)
  Pallas kernels  12.6 us (34%)
  waiting for transfers between devices  8.15 us (22%)
  other arithmetic  0.64 us (2%)
    ppermute x4, starting transfers between devices, on_device(): lax.ppermute(block, 'sub', [(k, (k + shift) % SUBS) for k in range(SUBS)])  8.83 us
    pallas_call x1, Pallas kernels, on_device(): kernel_call(own_kernel, [shape((NVEC, (TD + 2 * RIM) * TILE), bf16), shap...  6.18 us
    pallas_call x1, Pallas kernels, on_device(): kernel_call(main_kernel, [shape((COLS, COLS), f32), shape((COLS, 2 * RIM...  4.09 us
    ppermute x3, waiting for transfers between devices, on_device(): lax.ppermute(block, 'grp', [(k, k ^ 2 * step) for k in range(LAYERS)])  3.99 us
    ppermute x3, starting transfers between devices, on_device(): lax.ppermute(block, 'grp', [(k, k ^ 2 * step) for k in range(LAYERS)])  3.93 us
    ppermute x4, waiting for transfers between devices, on_device(): lax.ppermute(block, 'sub', [(k, (k + shift) % SUBS) for k in range(SUBS)])  2.18 us
    ppermute x1, waiting for transfers between devices, on_device(): lax.ppermute(other, 'grp', [(k, k ^ 1) for k in range(LAYERS)])  1.31 us
    pallas_call x1, Pallas kernels, on_device(): kernel_call(pack_kernel, [shape((NVEC, OV * TILE), bf16)] * 4 + [pltpu.VM...  1.17 us
  transfers between devices with their start and end apart: 10, of which 6 were waited for; matrix products, arithmetic and copies ran while one was open for 0% of the time, Pallas kernels for 28%

profile of v4, /device:TPU:16, one launch (start us, length us, event | category | flops | bytes accessed | tf_op | source)
XLA Modules:
  0.0 36.1 jit_solution(2999274061107316932)
XLA Ops:
  0.0 0.0 copy-start
  0.0 0.0 copy-start.1
  0.0 1.2 %shard_map.55 = (bf16[64,1024]{1,0:T(8,128)(2,1)S(1)}, bf16[64,1024]{1,0:T(8,128)(2,1)S(1)}, bf16[64,1024]{1,0:T(8,128)(2,1)S(1)}, bf16[64,1024]{1,0:T(8,128)(2,1)S(1)}, bf16[64,4096]{1,0:T(8,128)(2,1)S(1)}) custom-call(s32[3,32]{1,0:T(4,128)} %bitcast.23, s32[3,4,32]{2,1,0:T(4,128)} %bitcast.30, bf16[64,4096]{1,0:T(8,128)(2,1)} %bitcast.29), custom_call_target="tpu_custom_call" | custom-call | tf_op jit(solution)/shard_map/pallas_call | solution.py:204
  1.2 2.0 %collective-permute-start = (bf16[64,1024]{1,0:T(8,128)(2,1)S(1)}, bf16[64,1024]{1,0:T(8,128)(2,1)S(1)}, u32[]{:S(2)}, u32[]{:S(2)}) collective-permute-start(bf16[64,1024]{1,0:T(8,128)(2,1)S(1)} %get-tuple-element.27), channel_id=1, source_target_pairs={{0,8},{8,16},{16,24},{24,32},{32,40},{40,48},{48,56},{56,64},{64,7... | collective-permute-start | bytes 393224 | tf_op jit(solution)/shard_map/ppermute | solution.py:216
  3.2 3.3 %collective-permute-start.1 = (bf16[64,1024]{1,0:T(8,128)(2,1)S(1)}, bf16[64,1024]{1,0:T(8,128)(2,1)S(1)}, u32[]{:S(2)}, u32[]{:S(2)}) collective-permute-start(bf16[64,1024]{1,0:T(8,128)(2,1)S(1)} %get-tuple-element.28), channel_id=1, source_target_pairs={{0,16},{8,24},{16,32},{24,40},{32,48},{40,56},{48,64},{56,72},{64,... | collective-permute-start | bytes 393224 | tf_op jit(solution)/shard_map/ppermute | solution.py:216
  6.4 2.0 %collective-permute-start.2 = (bf16[64,1024]{1,0:T(8,128)(2,1)S(1)}, bf16[64,1024]{1,0:T(8,128)(2,1)S(1)}, u32[]{:S(2)}, u32[]{:S(2)}) collective-permute-start(bf16[64,1024]{1,0:T(8,128)(2,1)S(1)} %get-tuple-element.29), channel_id=1, source_target_pairs={{0,240},{8,248},{16,0},{24,8},{32,16},{40,24},{48,32},{56,40},{64,... | collective-permute-start | bytes 393224 | tf_op jit(solution)/shard_map/ppermute | solution.py:216
  8.5 1.5 %collective-permute-start.3 = (bf16[64,1024]{1,0:T(8,128)(2,1)S(1)}, bf16[64,1024]{1,0:T(8,128)(2,1)S(1)}, u32[]{:S(2)}, u32[]{:S(2)}) collective-permute-start(bf16[64,1024]{1,0:T(8,128)(2,1)S(1)} %get-tuple-element.30), channel_id=1, source_target_pairs={{0,248},{8,0},{16,8},{24,16},{32,24},{40,32},{48,40},{56,48},{64,5... | collective-permute-start | bytes 393224 | tf_op jit(solution)/shard_map/ppermute | solution.py:216
  10.0 6.2 %shard_map.56 = (bf16[64,5120]{1,0:T(8,128)(2,1)S(1)}, bf16[64,4096]{1,0:T(8,128)(2,1)S(1)}, bf16[16,5,256,256]{3,2,1,0:T(8,128)(2,1)S(1)}, bf16[256,4096]{1,0:T...) custom-call(bf16[16,5,256,256]{3,2,1,0:T(8,128)(2,1)} %bitcast.28, ...), custom_call_target="tpu_custom_call" | custom-call | flops 671088640 | bytes 16777216 | tf_op jit(solution)/shard_map/pallas_call | solution.py:221
  16.2 0.0 collective-permute-done.refs_0_.refs_2_
  16.2 0.0 collective-permute-done.1.refs_1_.refs_3_
  16.2 0.2 collective-permute-done.2.refs_2_.refs_4_
  16.4 2.0 %collective-permute-done.3.refs_3_.refs_5_ = bf16[64,1024]{1,0:T(8,128)(2,1)S(1)} collective-permute-done((bf16[64,1024]{1,0:T(8,128)(2,1)S(1)}, bf16[64,1024]{1,0:T(8,128)(2,1)S(1)}, u32[]{:S(2)}, u32[]{:S(2)}) %collective-permute-start.3) | collective-permute-done | bytes 131104 | tf_op jit(solution)/shard_map/ppermute | solution.py:216
  18.4 0.0 copy-done
  18.4 0.0 copy-done.1
  18.4 0.9 %shard_map.58 = (bf16[256,512]{1,0:T(8,128)(2,1)S(1)}, bf16[256,512]{1,0:T(8,128)(2,1)S(1)}) custom-call(s32[3,32]{1,0:T(4,128)S(1)} %bitcast.24, s32[3,1,4]{2,1,0:T(1,128)S(1)} %bitcast.26, bf16[256,512]{1,0:T(8,128)(2,1)S(1)} %get-tuple-element.33.refs_0_, ...), custom_call_target="tpu_custom_call", output_to_operand_aliasing={{0}: (2, {}), {1}: (3, {})} | custom-call | tf_op jit(solution)/shard_map/pallas_call | solution.py:239
  19.3 0.9 %collective-permute-start.4 = (bf16[256,512]{1,0:T(8,128)(2,1)S(1)}, bf16[256,512]{1,0:T(8,128)(2,1)S(1)}, u32[]{:S(2)}, u32[]{:S(2)}) collective-permute-start(bf16[256,512]{1,0:T(8,128)(2,1)S(1)} %get-tuple-element.35), channel_id=1, source_target_pairs={{0,8},{1,2},{2,1},{3,4},{4,3},{5,6},{6,5},{7,15},{8,0},{9,10},{10,... | collective-permute-start | bytes 786440 | tf_op jit(solution)/shard_map/ppermute | solution.py:245
  20.2 0.8 %collective-permute-start.5 = (bf16[256,512]{1,0:T(8,128)(2,1)S(1)}, bf16[256,512]{1,0:T(8,128)(2,1)S(1)}, u32[]{:S(2)}, u32[]{:S(2)}) collective-permute-start(bf16[256,512]{1,0:T(8,128)(2,1)S(1)} %get-tuple-element.36), channel_id=1, source_target_pairs={{0,1},{1,0},{2,3},{3,2},{4,5},{5,4},{6,7},{7,6},{8,9},{9,8},{10,11... | collective-permute-start | bytes 786440 | tf_op jit(solution)/shard_map/ppermute | solution.py:194
  21.0 4.1 %shard_map.57 = (f32[256,256]{1,0:T(8,128)S(1)}, bf16[256,1024]{1,0:T(8,128)(2,1)S(1)}, bf16[256,4096]{1,0:T(8,128)(2,1)S(1)}) custom-call(s32[3,32]{1,0:T(4,128)S(1)} %bitcast.25, s32[3,1,4]{2,1,0:T(1,128)S(1)} %bitcast.27, bf16[16,5,256,256]{3,2,1,0:T(8,128)(2,1)S(1)} %get-tuple-element.23.stiff, ...), custom_call_target="tpu_custom_call", output_to_operand_aliasing={{2}: (5, {})} | custom-call | flops 3221225472 | bytes 4194304 | tf_op jit(solution)/shard_map/pallas_call | solution.py:247
  25.1 0.7 %collective-permute-done.4.far = bf16[256,512]{1,0:T(8,128)(2,1)S(1)} collective-permute-done((bf16[256,512]{1,0:T(8,128)(2,1)S(1)}, bf16[256,512]{1,0:T(8,128)(2,1)S(1)}, u32[]{:S(2)}, u32[]{:S(2)}) %collective-permute-start.4) | collective-permute-done | bytes 262176 | tf_op jit(solution)/shard_map/ppermute | solution.py:245
  25.8 0.0 collective-permute-done.5.near
  25.8 0.3 shard_map.59
  26.1 0.1 collective-permute-start.6
  26.2 1.3 %collective-permute-done.6 = f32[4,32,256]{2,1,0:T(8,128)S(1)} collective-permute-done((f32[4,32,256]{2,1,0:T(8,128)S(1)}, f32[4,32,256]{2,1,0:T(8,128)S(1)}, u32[]{:S(2)}, u32[]{:S(2)}) %collective-permute-start.6) | collective-permute-done | bytes 131104 | tf_op jit(solution)/shard_map/ppermute | solution.py:265
  27.6 2.8 %collective-permute-start.7 = (f32[32,256]{1,0:T(8,128)S(1)}, f32[32,256]{1,0:T(8,128)S(1)}, u32[]{:S(2)}, u32[]{:S(2)}) collective-permute-start(f32[32,256]{1,0:T(8,128)S(1)} %get-tuple-element.39), channel_id=1, source_target_pairs={{0,4},{1,5},{2,6},{3,7},{4,0},{5,1},{6,2},{7,3},{8,12},{9,13},{10,... | collective-permute-start | bytes 98312 | tf_op jit(solution)/shard_map/ppermute | solution.py:270
  30.4 1.1 %collective-permute-start.8 = (f32[32,256]{1,0:T(8,128)S(1)}, f32[32,256]{1,0:T(8,128)S(1)}, u32[]{:S(2)}, u32[]{:S(2)}) collective-permute-start(f32[32,256]{1,0:T(8,128)S(1)} %get-tuple-element.41), channel_id=1, source_target_pairs={{0,6},{1,7},{2,4},{3,5},{4,2},{5,3},{6,0},{7,1},{8,14},{9,15},{10,... | collective-permute-start | bytes 98312 | tf_op jit(solution)/shard_map/ppermute | solution.py:270
  31.5 0.0 collective-permute-start.9
  31.5 1.6 %collective-permute-done.7 = f32[32,256]{1,0:T(8,128)S(1)} collective-permute-done((f32[32,256]{1,0:T(8,128)S(1)}, f32[32,256]{1,0:T(8,128)S(1)}, u32[]{:S(2)}, u32[]{:S(2)}) %collective-permute-start.7) | collective-permute-done | bytes 32800 | tf_op jit(solution)/shard_map/ppermute | solution.py:270
  33.1 2.4 %collective-permute-done.8 = f32[32,256]{1,0:T(8,128)S(1)} collective-permute-done((f32[32,256]{1,0:T(8,128)S(1)}, f32[32,256]{1,0:T(8,128)S(1)}, u32[]{:S(2)}, u32[]{:S(2)}) %collective-permute-start.8) | collective-permute-done | bytes 32800 | tf_op jit(solution)/shard_map/ppermute | solution.py:270
  35.5 0.0 collective-permute-done.9
  35.5 0.6 %fusion.2 = f32[1,32,256]{2,1,0:T(8,128)} fusion(f32[32,256]{1,0:T(8,128)S(1)} %collective-permute-done.9, f32[32,256]{1,0:T(8,128)S(1)} %collective-permute-done.8, f32[32,256]{1,0:T(8,128)S(1)} %collective-permute-done.7, f32[4,32,256]{2,1,0:T(8,128)S(1)} %add.25, s32[]{:T(128)S(6)} %select_n.13), kind=kLoop, calls=%fused_computation.3 | loop fusion | flops 24576 | bytes 163844 | tf_op jit(solution)/shard_map/broadcast_in_dim | solution.py:271
  (2 shorter events, 0.0 us)
Async XLA Ops:
  0.0 18.4 %copy-start = (s32[32,3]{0,1:T(4,128)S(1)}, s32[32,3]{0,1:T(4,128)}, u32[]{:S(2)}) copy-start(s32[32,3]{0,1:T(4,128)} %param.7) | copy-start | bytes 1156
  0.0 18.4 %copy-start.1 = (s32[1,1,3,4]{3,1,2,0:T(1,128)S(1)}, s32[1,1,3,4]{3,1,2,0:T(1,128)}, u32[]{:S(2)}) copy-start(s32[1,1,3,4]{3,1,2,0:T(1,128)} %param.9) | copy-start | bytes 148
  1.2 15.0 %collective-permute-start = (bf16[64,1024]{1,0:T(8,128)(2,1)S(1)}, bf16[64,1024]{1,0:T(8,128)(2,1)S(1)}, u32[]{:S(2)}, u32[]{:S(2)}) collective-permute-start(bf16[64,1024]{1,0:T(8,128)(2,1)S(1)} %get-tuple-element.27), channel_id=1, source_target_pairs={{0,8},{8,16},{16,24},{24,32},{32,40},{40,48},{48,56},{56,64},{64,7... | collective-permute-start | bytes 393224 | tf_op jit(solution)/shard_map/ppermute | solution.py:216
  3.2 13.0 %collective-permute-start.1 = (bf16[64,1024]{1,0:T(8,128)(2,1)S(1)}, bf16[64,1024]{1,0:T(8,128)(2,1)S(1)}, u32[]{:S(2)}, u32[]{:S(2)}) collective-permute-start(bf16[64,1024]{1,0:T(8,128)(2,1)S(1)} %get-tuple-element.28), channel_id=1, source_target_pairs={{0,16},{8,24},{16,32},{24,40},{32,48},{40,56},{48,64},{56,72},{64,... | collective-permute-start | bytes 393224 | tf_op jit(solution)/shard_map/ppermute | solution.py:216
  6.4 10.0 %collective-permute-start.2 = (bf16[64,1024]{1,0:T(8,128)(2,1)S(1)}, bf16[64,1024]{1,0:T(8,128)(2,1)S(1)}, u32[]{:S(2)}, u32[]{:S(2)}) collective-permute-start(bf16[64,1024]{1,0:T(8,128)(2,1)S(1)} %get-tuple-element.29), channel_id=1, source_target_pairs={{0,240},{8,248},{16,0},{24,8},{32,16},{40,24},{48,32},{56,40},{64,... | collective-permute-start | bytes 393224 | tf_op jit(solution)/shard_map/ppermute | solution.py:216
  8.5 9.9 %collective-permute-start.3 = (bf16[64,1024]{1,0:T(8,128)(2,1)S(1)}, bf16[64,1024]{1,0:T(8,128)(2,1)S(1)}, u32[]{:S(2)}, u32[]{:S(2)}) collective-permute-start(bf16[64,1024]{1,0:T(8,128)(2,1)S(1)} %get-tuple-element.30), channel_id=1, source_target_pairs={{0,248},{8,0},{16,8},{24,16},{32,24},{40,32},{48,40},{56,48},{64,5... | collective-permute-start | bytes 393224 | tf_op jit(solution)/shard_map/ppermute | solution.py:216
  19.3 6.5 %collective-permute-start.4 = (bf16[256,512]{1,0:T(8,128)(2,1)S(1)}, bf16[256,512]{1,0:T(8,128)(2,1)S(1)}, u32[]{:S(2)}, u32[]{:S(2)}) collective-permute-start(bf16[256,512]{1,0:T(8,128)(2,1)S(1)} %get-tuple-element.35), channel_id=1, source_target_pairs={{0,8},{1,2},{2,1},{3,4},{4,3},{5,6},{6,5},{7,15},{8,0},{9,10},{10,... | collective-permute-start | bytes 786440 | tf_op jit(solution)/shard_map/ppermute | solution.py:245
  20.2 5.6 %collective-permute-start.5 = (bf16[256,512]{1,0:T(8,128)(2,1)S(1)}, bf16[256,512]{1,0:T(8,128)(2,1)S(1)}, u32[]{:S(2)}, u32[]{:S(2)}) collective-permute-start(bf16[256,512]{1,0:T(8,128)(2,1)S(1)} %get-tuple-element.36), channel_id=1, source_target_pairs={{0,1},{1,0},{2,3},{3,2},{4,5},{5,4},{6,7},{7,6},{8,9},{9,8},{10,11... | collective-permute-start | bytes 786440 | tf_op jit(solution)/shard_map/ppermute | solution.py:194
  26.1 1.4 %collective-permute-start.6 = (f32[4,32,256]{2,1,0:T(8,128)S(1)}, f32[4,32,256]{2,1,0:T(8,128)S(1)}, u32[]{:S(2)}, u32[]{:S(2)}) collective-permute-start(f32[4,32,256]{2,1,0:T(8,128)S(1)} %get-tuple-element.38), channel_id=1, source_target_pairs={{0,1},{1,0},{2,3},{3,2},{4,5},{5,4},{6,7},{7,6},{8,9},{9,8},{10,11... | collective-permute-start | bytes 393224 | tf_op jit(solution)/shard_map/ppermute | solution.py:265
  27.6 5.5 %collective-permute-start.7 = (f32[32,256]{1,0:T(8,128)S(1)}, f32[32,256]{1,0:T(8,128)S(1)}, u32[]{:S(2)}, u32[]{:S(2)}) collective-permute-start(f32[32,256]{1,0:T(8,128)S(1)} %get-tuple-element.39), channel_id=1, source_target_pairs={{0,4},{1,5},{2,6},{3,7},{4,0},{5,1},{6,2},{7,3},{8,12},{9,13},{10,... | collective-permute-start | bytes 98312 | tf_op jit(solution)/shard_map/ppermute | solution.py:270
  30.4 5.1 %collective-permute-start.8 = (f32[32,256]{1,0:T(8,128)S(1)}, f32[32,256]{1,0:T(8,128)S(1)}, u32[]{:S(2)}, u32[]{:S(2)}) collective-permute-start(f32[32,256]{1,0:T(8,128)S(1)} %get-tuple-element.41), channel_id=1, source_target_pairs={{0,6},{1,7},{2,4},{3,5},{4,2},{5,3},{6,0},{7,1},{8,14},{9,15},{10,... | collective-permute-start | bytes 98312 | tf_op jit(solution)/shard_map/ppermute | solution.py:270
  31.5 4.0 %collective-permute-start.9 = (f32[32,256]{1,0:T(8,128)S(1)}, f32[32,256]{1,0:T(8,128)S(1)}, u32[]{:S(2)}, u32[]{:S(2)}) collective-permute-start(f32[32,256]{1,0:T(8,128)S(1)} %get-tuple-element.40), channel_id=1, source_target_pairs={{0,2},{1,3},{2,0},{3,1},{4,6},{5,7},{6,4},{7,5},{8,10},{9,11},{10,... | collective-permute-start | bytes 98312 | tf_op jit(solution)/shard_map/ppermute | solution.py:270
